TPU v7x, 128 devices: a whole 4x4x4 slice. The times are simulated.
128 devices in a mesh: leaf: 8 (over z, core), seq: 16 (over y, x).
Axes of the slice: x: 4, y: 4, z: 4, core: 2. Of those that a mesh axis runs over, the one named last changes fastest.
Arguments:
- hidden_in: bfloat16 [32768, 5120], P(('leaf', 'seq')), parts along dimension 0, may hold values from -6 to 6
- queries: bfloat16 [32768, 1024], P(('leaf', 'seq')), parts along dimension 0, may hold values from -32 to 32
- keys: bfloat16 [32768, 128], P(('leaf', 'seq')), parts along dimension 0, may hold values from -4 to 4
- values: bfloat16 [32768, 128], P(('leaf', 'seq')), parts along dimension 0, may hold values from -6 to 6
- out_grad: bfloat16 [32768, 1024], P(('leaf', 'seq')), parts along dimension 0, may hold values from -6 to 6
- parents: int32 [256], P('leaf'), parts along dimension 0, may hold values from -1 to 30, as said below
Outputs:
- query_grad: bfloat16 [32768, 1024], P(('leaf', 'seq')), parts along dimension 0
- proj_grad: float32 [40960, 256], P(('leaf', 'seq')), parts along dimension 0
There are 8 independent parts, one for each index of `leaf`. A program takes and returns all parts, laid end to end along the dimension named above; each array names one. Nothing has to cross between parts.
Inputs may be any that keep to these rules, and one draw needn't show every extreme that they name: Segments are in depth-first order: a parent is an earlier segment. Following parents from any segment passes at most 16 segments before a root, and exactly 16 for some segment.
All inputs are finite; a program needn't handle non-finite values.
Results may differ from a plain program's by a relative error of at most 0.006.
Values may be sent and summed in bfloat16 or wider, within the bound.
A program may use at most 128 MiB of HBM per device.

v0:
```python
import jax
import jax.numpy as jnp
from jax import lax
from jax.sharding import PartitionSpec as P

SEG = 128


start_level = -1e30


def ancestry(parents):
    count = parents.shape[0]
    indices = jnp.arange(count, dtype=jnp.int32)
    reach = (parents[:, None] == indices[None, :]).astype(jnp.float32)
    for doubling in range(count.bit_length()):
        reach = jnp.minimum(reach + jnp.dot(reach, reach, precision=lax.Precision.HIGHEST), 1.0)
    return reach > 0.5


def pair_mask(ancestors, query_start, query_count, key_start, key_count, seg_len):
    query_first = jnp.asarray(query_start)
    key_first = jnp.asarray(key_start)
    query_segs = query_count // seg_len
    key_segs = key_count // seg_len
    coarse = lax.dynamic_slice(
        ancestors, (query_first // seg_len, key_first // seg_len), (query_segs, key_segs)
    )
    coarse = jnp.broadcast_to(
        coarse[:, None, :, None], (query_segs, seg_len, key_segs, seg_len)
    ).reshape(query_count, key_count)
    query_pos = query_first + jnp.arange(query_count, dtype=jnp.int32)
    key_pos = key_first + jnp.arange(key_count, dtype=jnp.int32)
    same_seg = query_pos[:, None] // seg_len == key_pos[None, :] // seg_len
    return coarse | same_seg & (key_pos[None, :] <= query_pos[:, None])


def masked_scores(query_heads, key_rows, mask, scale):
    raw = (
        jnp.einsum("qgd,kd->gqk", query_heads, key_rows, preferred_element_type=jnp.float32) * scale
    )
    return jnp.where(mask[None], raw, -jnp.inf)


def gated(live_fn, carry):
    result = live_fn(carry)
    return result


def on_device(hidden_in, queries, keys, values, out_grad, parents):
    seq_count = lax.axis_size("seq")
    rank = lax.axis_index("seq")
    local_len, head_width = keys.shape
    group = queries.shape[1] // head_width
    total_len = local_len * seq_count
    scale = head_width ** (-0.5)
    ancestors = ancestry(parents)
    own_start = rank * local_len
    block_len = min(total_len, 1024)
    block_count = total_len // block_len
    key_all, value_all = (
        lax.all_gather(keys, "seq", axis=0, tiled=True),
        lax.all_gather(values, "seq", axis=0, tiled=True),
    )
    query_heads = queries.reshape(local_len, group, head_width)
    grad_heads = out_grad.reshape(local_len, group, head_width)

    def key_block(index):
        key_start = (index * block_len).astype(jnp.int32)
        key_rows = lax.dynamic_slice_in_dim(key_all, key_start, block_len, 0)
        value_rows = lax.dynamic_slice_in_dim(value_all, key_start, block_len, 0)
        mask = pair_mask(ancestors, own_start, local_len, key_start, block_len, SEG)
        return (key_rows, value_rows, mask)

    def stat_step(index, carry):
        key_rows, value_rows, mask = key_block(index)

        def stat_live(state):
            run_max, run_sum = state
            scores = masked_scores(query_heads, key_rows, mask, scale)
            new_max = jnp.maximum(run_max, jnp.max(scores, axis=-1))
            new_sum = run_sum * jnp.exp(run_max - new_max) + jnp.sum(
                jnp.exp(scores - new_max[..., None]), axis=-1
            )
            return (new_max, new_sum)

        return gated(stat_live, carry)

    init = (
        jnp.full((group, local_len), start_level, jnp.float32),
        jnp.zeros((group, local_len), jnp.float32),
    )
    run_max, run_sum = lax.fori_loop(0, block_count, stat_step, init)
    log_total = run_max + jnp.log(run_sum)

    def output_step(index, carry):
        key_rows, value_rows, mask = key_block(index)

        def output_live(total):
            probs = jnp.exp(
                masked_scores(query_heads, key_rows, mask, scale) - log_total[..., None]
            )
            return total + jnp.einsum(
                "gqk,kd->qgd",
                probs.astype(jnp.bfloat16),
                value_rows,
                preferred_element_type=jnp.float32,
            )

        return gated(output_live, carry)

    attended = lax.fori_loop(
        0, block_count, output_step, jnp.zeros((local_len, group, head_width), jnp.float32)
    )
    delta = jnp.sum(grad_heads.astype(jnp.float32) * attended, axis=-1).T

    def grad_step(carry, index):
        key_rows, value_rows, mask = key_block(index)

        def grad_live(query_acc):
            probs = jnp.exp(
                masked_scores(query_heads, key_rows, mask, scale) - log_total[..., None]
            )
            probs_low = probs.astype(jnp.bfloat16)
            dprobs = jnp.einsum(
                "qgd,kd->gqk", grad_heads, value_rows, preferred_element_type=jnp.float32
            )
            dscores = (probs * (dprobs - delta[..., None])).astype(jnp.bfloat16)
            query_acc = query_acc + jnp.einsum(
                "gqk,kd->qgd", dscores, key_rows, preferred_element_type=jnp.float32
            )
            key_part = (
                jnp.einsum("gqk,qgd->kd", dscores, query_heads, preferred_element_type=jnp.float32)
                * scale
            )
            value_part = jnp.einsum(
                "gqk,qgd->kd", probs_low, grad_heads, preferred_element_type=jnp.float32
            )
            return (query_acc, jnp.concatenate([key_part, value_part], axis=-1))

        return gated(grad_live, carry)

    query_acc, pieces = lax.scan(
        grad_step,
        jnp.zeros((local_len, group, head_width), jnp.float32),
        jnp.arange(block_count, dtype=jnp.int32),
    )
    result = pieces.reshape((total_len,) + pieces.shape[2:])
    kv_grad = lax.psum_scatter(result, "seq", scatter_dimension=0, tiled=True)
    query_grad = (query_acc * scale).reshape(local_len, group * head_width).astype(jnp.bfloat16)
    kv_low = kv_grad.astype(jnp.bfloat16)
    proj_grad = lax.psum_scatter(
        lax.dot_general(
            hidden_in, kv_low, (((0,), (0,)), ((), ())), preferred_element_type=jnp.float32
        ),
        "seq",
        scatter_dimension=0,
        tiled=True,
    )
    return (query_grad, proj_grad)


def solution(mesh):
    in_specs = (
        P(("leaf", "seq"), None),
        P(("leaf", "seq"), None),
        P(("leaf", "seq"), None),
        P(("leaf", "seq"), None),
        P(("leaf", "seq"), None),
        P("leaf"),
    )
    out_specs = (P(("leaf", "seq"), None), P(("leaf", "seq"), None))
    return jax.shard_map(
        on_device, mesh=mesh, in_specs=in_specs, out_specs=out_specs, check_vma=False
    )
```

profile of v0, /device:TPU:0, one launch (start us, length us, event | category | flops | bytes accessed | tf_op | source)
XLA Modules:
  0.0 386.7 jit_solution(13512158879394953286)
XLA Ops:
  10.5 2.1 copy.69
  14.8 40.4 %all-gather.3.cloned.1.call-done = bf16[4096,128]{1,0:T(8,128)(2,1)} async-done(((bf16[256,128]{1,0:T(8,128)(2,1)}), bf16[4096,128]{1,0:T(8,128)(2,1)}) %all-gather.3.cloned.1.call-update) | async-done | bytes 1048592 | tf_op jit(solution)/shard_map/all_gather | solution.py:62
  55.2 21.3 %while.52 = (s32[]{:T(128)}, f32[8,256]{1,0:T(8,128)S(1)}, f32[8,256]{1,0:T(8,128)S(1)}, pred[32,32]{1,0:T(8,128)(4,1)S(1)}, s32[]{:T(128)}, /*index=5*/s32[]{:T...) while((s32[]{:T(128)}, f32[8,256]{1,0:T(8,128)S(1)}, ...), condition=%wide.region_3.4_spmd.clone, body=%wide.region_0.3_spmd.clone.sunk | while | flops 552630272 | bytes 19526084 | solution.py:93
  56.3 2.5 fusion.116
  58.8 1.7 exponential_reduce_fusion.2
  61.6 2.5 fusion.116
  64.1 1.7 exponential_reduce_fusion.2
  67.0 2.5 fusion.116
  69.4 1.7 exponential_reduce_fusion.2
  72.3 2.5 fusion.116
  74.8 1.7 exponential_reduce_fusion.2
  76.5 22.7 %all-gather.5.cloned.1.call-done = bf16[4096,128]{1,0:T(8,128)(2,1)} async-done(((bf16[256,128]{1,0:T(8,128)(2,1)}), bf16[4096,128]{1,0:T(8,128)(2,1)}) %all-gather.5.cloned.1.call-update) | async-done | bytes 1048592 | tf_op jit(solution)/shard_map/all_gather | solution.py:63
  99.2 27.2 %while.53 = (s32[]{:T(128)}, f32[256,8,128]{0,2,1:T(8,128)}, bf16[4096,128]{1,0:T(8,128)(2,1)}, pred[32,32]{1,0:T(8,128)(4,1)S(1)}, s32[]{:T(128)}, /*index=5*/s...) while((s32[]{:T(128)}, f32[256,8,128]{0,2,1:T(8,128)}, ...), condition=%wide.region_5.6_spmd.clone, body=%wide.region_4.5_spmd.clone.sunk | while | flops 1083723776 | bytes 4749255 | solution.py:112
  100.9 4.9 %fusion.122 = f32[256,8,128]{0,2,1:T(8,128)} fusion(f32[8,256]{1,0:T(8,128)S(1)} %get-tuple-element.1386, pred[256,1024]{0,1:T(8,128)(4,1)} %copy.106, bf16[256,8,128]{2,0,1:T(8,128)(2,1)} %get-tuple-element.1385, f32[256,8,128]{0,2,1:T(8,128)} %get-tuple-element.1362, pred[]{:T(512)S(6)} %compare.159, bf16[4096,128]{1,0:T(8,128)(2,1)} %get-tuple-element.1384, ...), kind=kOutput, calls=%fused_computation.33.clone.1 | convolution fusion | flops 1082654720 | bytes 3417600 | tf_op jit(solution)/shard_map/while/body/eval_jaxpr/gqk,kd->qgd/dot_general | solution.py:103
  107.4 5.2 %fusion.122 = f32[256,8,128]{0,2,1:T(8,128)} fusion(f32[8,256]{1,0:T(8,128)S(1)} %get-tuple-element.1386, pred[256,1024]{0,1:T(8,128)(4,1)} %copy.106, bf16[256,8,128]{2,0,1:T(8,128)(2,1)} %get-tuple-element.1385, f32[256,8,128]{0,2,1:T(8,128)} %get-tuple-element.1362, pred[]{:T(512)S(6)} %compare.159, bf16[4096,128]{1,0:T(8,128)(2,1)} %get-tuple-element.1384, ...), kind=kOutput, calls=%fused_computation.33.clone.1 | convolution fusion | flops 1082654720 | bytes 3417600 | tf_op jit(solution)/shard_map/while/body/eval_jaxpr/gqk,kd->qgd/dot_general | solution.py:103
  114.3 5.2 %fusion.122 = f32[256,8,128]{0,2,1:T(8,128)} fusion(f32[8,256]{1,0:T(8,128)S(1)} %get-tuple-element.1386, pred[256,1024]{0,1:T(8,128)(4,1)} %copy.106, bf16[256,8,128]{2,0,1:T(8,128)(2,1)} %get-tuple-element.1385, f32[256,8,128]{0,2,1:T(8,128)} %get-tuple-element.1362, pred[]{:T(512)S(6)} %compare.159, bf16[4096,128]{1,0:T(8,128)(2,1)} %get-tuple-element.1384, ...), kind=kOutput, calls=%fused_computation.33.clone.1 | convolution fusion | flops 1082654720 | bytes 3417600 | tf_op jit(solution)/shard_map/while/body/eval_jaxpr/gqk,kd->qgd/dot_general | solution.py:103
  121.2 5.2 %fusion.122 = f32[256,8,128]{0,2,1:T(8,128)} fusion(f32[8,256]{1,0:T(8,128)S(1)} %get-tuple-element.1386, pred[256,1024]{0,1:T(8,128)(4,1)} %copy.106, bf16[256,8,128]{2,0,1:T(8,128)(2,1)} %get-tuple-element.1385, f32[256,8,128]{0,2,1:T(8,128)} %get-tuple-element.1362, pred[]{:T(512)S(6)} %compare.159, bf16[4096,128]{1,0:T(8,128)(2,1)} %get-tuple-element.1384, ...), kind=kOutput, calls=%fused_computation.33.clone.1 | convolution fusion | flops 1082654720 | bytes 3417600 | tf_op jit(solution)/shard_map/while/body/eval_jaxpr/gqk,kd->qgd/dot_general | solution.py:103
  127.9 86.8 %while.54 = (s32[]{:T(128)}, f32[256,8,128]{0,2,1:T(8,128)}, f32[4,1024,256]{2,1,0:T(8,128)}, s32[4]{0:T(128)S(1)}, bf16[4096,128]{1,0:T(8,128)(2,1)}, /*index=5...) while((s32[]{:T(128)}, f32[256,8,128]{0,2,1:T(8,128)}, ...), condition=%wide.region_8.9_spmd.clone, body=%wide.region_7.8_spmd.clone.sunk | while | flops 2707312640 | bytes 63484528 | solution.py:143
  131.0 2.3 fusion.133
  133.3 2.4 fusion.136
  135.7 3.8 fusion.134
  139.5 1.5 fusion.137
  141.0 1.9 fusion.135
  144.9 2.6 copy.109
  147.5 2.3 constant_dynamic-update-slice_fusion.2
  152.7 2.3 fusion.133
  155.0 2.4 fusion.136
  157.4 3.8 fusion.134
  161.1 1.5 fusion.137
  162.6 1.9 fusion.135
  166.6 2.6 copy.109
  169.1 2.3 constant_dynamic-update-slice_fusion.2
  174.4 2.3 fusion.133
  176.6 2.4 fusion.136
  179.0 3.8 fusion.134
  184.3 1.9 fusion.135
  188.2 2.6 copy.109
  190.8 2.3 constant_dynamic-update-slice_fusion.2
  196.0 2.3 fusion.133
  198.3 2.4 fusion.136
  200.7 3.8 fusion.134
  205.9 1.9 fusion.135
  209.9 2.6 copy.109
  212.4 2.3 constant_dynamic-update-slice_fusion.2
  214.8 76.9 %reduce-scatter.5.cloned.1.call-done = f32[256,256]{1,0:T(8,128)} async-done(((f32[4096,256]{1,0:T(8,128)}), f32[256,256]{1,0:T(8,128)}) %reduce-scatter.5.cloned.1.call-update) | async-done | bytes 262160 | tf_op jit(solution)/shard_map/reduce_scatter | solution.py:149
  291.7 4.1 %convolution_bitcast_fusion.2 = f32[5120,256]{0,1:T(8,128)} fusion(bf16[256,5120]{1,0:T(8,128)(2,1)S(1)} %copy-done, f32[256,256]{1,0:T(8,128)} %reduce-scatter.5.cloned.1.call-done), kind=kOutput, calls=%fused_computation.99 | convolution fusion | flops 671154176 | bytes 8126464 | tf_op jit(solution)/shard_map/dot_general | solution.py:153
  295.9 6.0 %copy.84 = f32[5120,256]{1,0:T(8,128)} copy(f32[5120,256]{0,1:T(8,128)} %convolution_bitcast_fusion.2) | data formatting | bytes 10485760
  304.2 76.0 %reduce-scatter.7.cloned.1.call-done = f32[320,256]{1,0:T(8,128)} async-done(((f32[5120,256]{1,0:T(8,128)}), f32[320,256]{1,0:T(8,128)}) %reduce-scatter.7.cloned.1.call-update) | async-done | bytes 327696
  (158 shorter events, 40.4 us)
Async XLA Ops:
  7.2 284.6 %copy-start = (bf16[256,5120]{1,0:T(8,128)(2,1)S(1)}, bf16[256,5120]{1,0:T(8,128)(2,1)}, u32[]{:S(2)}) copy-start(bf16[256,5120]{1,0:T(8,128)(2,1)} %param.12) | copy-start | bytes 7864324
  7.2 48.0 %all-gather.3.cloned.1.call-start = ((), (), s32[]{:S(2)}) async-start(), calls=%async_computation.2 | async-start | bytes 1114112 | tf_op jit(solution)/shard_map/all_gather | solution.py:62
  7.9 91.3 %all-gather.5.cloned.1.call-start = ((), (), s32[]{:S(2)}) async-start(), calls=%async_computation.3 | async-start | bytes 1114112 | tf_op jit(solution)/shard_map/all_gather | solution.py:63
  8.7 283.1 %reduce-scatter.5.cloned.1.call-start = ((), (), s32[]{:S(2)}) async-start(), calls=%async_computation.4 | async-start | bytes 4456448 | tf_op jit(solution)/shard_map/reduce_scatter | solution.py:149
  13.8 41.4 %copy-start.3 = (bf16[256,1024]{0,1:T(8,128)(2,1)}, bf16[256,1024]{0,1:T(8,128)(2,1)S(1)}, u32[]{:S(2)}) copy-start(bf16[256,1024]{0,1:T(8,128)(2,1)S(1)} %copy.67) | copy-start | bytes 1572868
  99.2 28.7 %copy-start.4 = (bf16[256,1024]{0,1:T(8,128)(2,1)S(1)}, bf16[256,1024]{0,1:T(8,128)(2,1)}, u32[]{:S(2)}) copy-start(bf16[256,1024]{0,1:T(8,128)(2,1)} %copy-done.3) | copy-start | bytes 1572868
  131.0 2.3 copy-start.5
  131.0 2.3 copy-start.6
  135.7 5.3 %copy-start.1 = (f32[256,8,128]{0,2,1:T(8,128)S(1)}, f32[256,8,128]{0,2,1:T(8,128)}, u32[]{:S(2)}) copy-start(f32[256,8,128]{0,2,1:T(8,128)} %get-tuple-element.1417) | copy-start | bytes 3145732 | tf_op jit(solution)/shard_map/while
  142.8 1.0 copy-start.2
  152.7 2.3 copy-start.5
  152.7 2.3 copy-start.6
  157.3 5.3 %copy-start.1 = (f32[256,8,128]{0,2,1:T(8,128)S(1)}, f32[256,8,128]{0,2,1:T(8,128)}, u32[]{:S(2)}) copy-start(f32[256,8,128]{0,2,1:T(8,128)} %get-tuple-element.1417) | copy-start | bytes 3145732 | tf_op jit(solution)/shard_map/while
  164.5 1.0 copy-start.2
  174.4 2.3 copy-start.5
  174.4 2.3 copy-start.6
  179.0 5.3 %copy-start.1 = (f32[256,8,128]{0,2,1:T(8,128)S(1)}, f32[256,8,128]{0,2,1:T(8,128)}, u32[]{:S(2)}) copy-start(f32[256,8,128]{0,2,1:T(8,128)} %get-tuple-element.1417) | copy-start | bytes 3145732 | tf_op jit(solution)/shard_map/while
  186.2 1.0 copy-start.2
  196.0 2.3 copy-start.5
  196.0 2.3 copy-start.6
  200.7 5.3 %copy-start.1 = (f32[256,8,128]{0,2,1:T(8,128)S(1)}, f32[256,8,128]{0,2,1:T(8,128)}, u32[]{:S(2)}) copy-start(f32[256,8,128]{0,2,1:T(8,128)} %get-tuple-element.1417) | copy-start | bytes 3145732 | tf_op jit(solution)/shard_map/while
  207.8 1.0 copy-start.2
  214.7 165.4 %reduce-scatter.7.cloned.1.call-start = ((), (), s32[]{:S(2)}) async-start(), calls=%async_computation.5 | async-start | bytes 5570560
Sparse Core Ops, SparseCore 0:
  10.2 45.0 all-gather.2
  57.4 41.8 all-gather.4
  214.9 76.8 reduce-scatter.4
  302.0 78.1 reduce-scatter.6
where the time goes:
time: 388 us; the launch traced here: 387 us
  waiting for transfers between devices  217 us (56%)
  matrix products  83.1 us (21%)
  local copies, waits for them, and re-layouts  49.9 us (13%)
  other arithmetic  18.6 us (5%)
  between operations  13.9 us (4%)
    unnamed x5, waiting for transfers between devices  77.4 us
    reduce_scatter x1, waiting for transfers between devices, on_device(): kv_grad = lax.psum_scatter(result, 'seq', scatter_dimension=0, tiled=True)  76.9 us
    all_gather x1, waiting for transfers between devices, on_device(): lax.all_gather(keys, 'seq', axis=0, tiled=True)  40.4 us
    all_gather x1, waiting for transfers between devices, on_device(): lax.all_gather(values, 'seq', axis=0, tiled=True)  22.7 us
    dot_general x4, matrix products, output_live(): jnp.einsum('gqk,kd->qgd', probs.astype(jnp.bfloat16), value_rows, preferr...  20.5 us
    dynamic_update_slice x8, local copies, waits for them, and re-layouts, on_device(): lax.scan(grad_step, jnp.zeros((local_len, group, head_width), jnp.float32...  19.4 us
    dot_general x8, matrix products, masked_scores(): jnp.einsum('qgd,kd->gqk', query_heads, key_rows, preferred_element_type=j...  18.8 us
    dot_general x4, matrix products, grad_live(): jnp.einsum('qgd,kd->gqk', grad_heads, value_rows, preferred_element_type=...  15.1 us
  transfers between devices with their start and end apart: 4, of which 4 were waited for; matrix products, arithmetic and copies ran while one was open for 8% of the time, Pallas kernels for 0%

commit v1 on v0

v1 whole, which is shorter than its diff:
```python
import functools

import jax
import jax.numpy as jnp
from jax import lax
from jax.experimental import pallas as pl
from jax.experimental.pallas import tpu as pltpu
from jax.sharding import PartitionSpec as P

BF, F32 = jnp.bfloat16, jnp.float32
MESH = pl.DeviceIdType.MESH
SIDE = 4
RANKS = SIDE * SIDE
SEG, HD, GROUP = 128, 128, 8
SEGS = 2 * RANKS
DEPTH = 16
SLOTS = DEPTH + 1
KEYS = SLOTS * SEG
PAIRS = GROUP // 2
UNITS = 2 * PAIRS
W = 2 * SEG
MC = 544
D = 5120
DCOLS = D // RANKS
LOG2E = 1.4426950408889634
SCALE = HD ** -0.5
PEN = 1e30
STEPS = (1, 3, 2)


def dot(a, b):
    return jnp.dot(a, b, preferred_element_type=F32)


def place():
    me = lax.axis_index("seq")
    return me, me // SIDE, lax.rem(me, SIDE)


def at(dy, dx):
    _, y, x = place()
    return lax.rem(y + dy + SIDE, SIDE) * SIDE + lax.rem(x + dx + SIDE, SIDE)


def remote(src, dst, send, recv, rank):
    return pltpu.make_async_remote_copy(
        src, dst, send, recv, device_id={"seq": rank}, device_id_type=MESH
    )


def loop(count, body):
    def step(index, carry):
        body(index)
        return carry

    lax.fori_loop(0, count, step, 0)


def score_unit(u, kc, qt, e, mxs):
    t = u // PAIRS
    weights = qt[u]
    key = lax.broadcasted_iota(jnp.int32, (SEG, W), 0)
    row = lax.broadcasted_iota(jnp.int32, (SEG, W), 1)
    row = jnp.where(row >= SEG, row - SEG, row)
    mx = jnp.full((8, W), -3e38, F32)
    for start in range(0, KEYS, MC):
        s = dot(kc[t, pl.ds(start, MC), :], weights)
        if start + MC == KEYS:
            own = jnp.where(key <= row, s[MC - SEG :], -PEN)
            s = jnp.concatenate([s[: MC - SEG], own], axis=0)
        e[u, pl.ds(start, MC), :] = s
        mx = jnp.maximum(mx, jnp.max(s.reshape(MC // 8, 8, W), axis=0))
    mxs[u] = mx


def prob_unit(u, slots, e, mxs, inv, p):
    t = u // PAIRS
    m = jnp.max(mxs[u], axis=0, keepdims=True) * (SCALE * LOG2E)
    acc = jnp.zeros((8, W), F32)
    for i in range(SLOTS):
        rows = pl.ds(i * SEG, SEG)
        shift = m
        if i < DEPTH:
            shift = m + jnp.where(slots[t, i] == SEGS, jnp.float32(PEN), jnp.float32(0.0))
        x = jnp.exp2(e[u, rows, :] * (SCALE * LOG2E) - shift)
        e[u, rows, :] = x
        acc = acc + jnp.sum(x.reshape(SEG // 8, 8, W), axis=0)
    r = 1.0 / jnp.sum(acc, axis=0, keepdims=True)
    inv[u] = jnp.broadcast_to(r, (8, W))
    for i in range(SLOTS):
        rows = pl.ds(i * SEG, SEG)
        p[u, rows, :] = (e[u, rows, :] * r).astype(BF)


def delta_unit(u, vct, gt, p, delta):
    o = dot(vct[u // PAIRS], p[u])
    d = jnp.sum(gt[u].astype(F32) * o, axis=0, keepdims=True)
    delta[u] = jnp.broadcast_to(d, (8, W))


def side_grad(t, lhs, rhs, acc):
    total = dot(lhs[t * PAIRS], rhs[t * PAIRS])
    for h in range(1, PAIRS):
        total += dot(lhs[t * PAIRS + h], rhs[t * PAIRS + h])
    acc[t, pl.ds(0, SLOTS)] = total.reshape(SLOTS, SEG, HD)
    acc[t, SLOTS] = jnp.zeros((SEG, HD), F32)


def ds_unit(u, vc, gt, e, inv, delta, ds):
    t = u // PAIRS
    weights = gt[u]
    r = inv[u, 0:1, :]
    d = delta[u, 0:1, :]
    for start in range(0, KEYS, MC):
        rows = pl.ds(start, MC)
        dp = dot(vc[t, rows, :], weights)
        ds[u, rows, :] = (e[u, rows, :] * r * (dp - d)).astype(BF)


def dq_unit(u, kct, ds, dq):
    t = u // PAIRS
    g = (dot(kct[t], ds[u]) * SCALE).T.astype(BF)
    first = lax.rem(u, PAIRS) * W
    rows = pl.ds(pl.multiple_of(t * SEG, SEG), SEG)
    for k in range(2):
        dq[rows, pl.ds(pl.multiple_of(first + k * HD, HD), HD)] = g[k * SEG : (k + 1) * SEG]


class Gather:
    def __init__(self, buf, send, recv):
        self.buf, self.send, self.recv = buf, send, recv
        self.copies = {}

    def shift(self, half, first, second):
        return at(second, first) if half == 0 else at(first, second)

    def start(self, half, p, q, to_p, to_q):
        origin = 2 * self.shift(half, -p, -q) + half
        target = self.shift(half, to_p - p, to_q - q)
        sem = (half, to_p * SIDE + to_q)
        copy = remote(
            self.buf.at[origin], self.buf.at[origin], self.send.at[sem], self.recv.at[sem], target
        )
        copy.start()
        self.copies[half, to_p, to_q] = copy

    def own(self):
        for step in STEPS:
            for half in range(2):
                self.start(half, 0, 0, step, 0)
        for step in STEPS:
            for half in range(2):
                self.start(half, 0, 0, 0, step)

    def forward(self):
        for p in STEPS:
            for half in range(2):
                self.copies[half, p, 0].wait_recv()
                for q in STEPS:
                    self.start(half, p, 0, p, q)

    def arrive(self):
        for (half, p, q), copy in self.copies.items():
            if q:
                copy.wait_recv()

    def drain(self):
        for copy in self.copies.values():
            copy.wait_send()


class Reduce:
    def __init__(self, stage, got, mid, last, send, recv):
        self.stage, self.got, self.mid, self.last = stage, got, mid, last
        self.send, self.recv = send, recv
        self.first, self.second = {}, {}

    def put(self, dest, low, high):
        y, x = dest // SIDE, lax.rem(dest, SIDE)
        self.stage[0, x, y] = low.astype(BF)
        self.stage[1, y, x] = high.astype(BF)

    def start(self):
        _, y, x = place()
        for step in STEPS:
            for half in range(2):
                column = lax.rem((x, y)[half] + step, SIDE)
                target = (at(0, step), at(step, 0))[half]
                self.first[half, step] = remote(
                    self.stage.at[half, column],
                    self.got.at[half, step - 1],
                    self.send.at[half, 0, step],
                    self.recv.at[half, 0, step],
                    target,
                )
                self.first[half, step].start()

    def middle(self):
        _, y, x = place()
        for half in range(2):
            for step in STEPS:
                self.first[half, step].wait_recv()
            here = (x, y)[half]
            for k in range(SIDE):
                total = self.stage[half, here, k].astype(F32)
                for step in STEPS:
                    total += self.got[half, step - 1, k].astype(F32)
                self.mid[half, k] = total.astype(BF)
            for step in STEPS:
                row = lax.rem((y, x)[half] + step, SIDE)
                target = (at(step, 0), at(0, step))[half]
                self.second[half, step] = remote(
                    self.mid.at[half, row],
                    self.last.at[half, step - 1],
                    self.send.at[half, 1, step],
                    self.recv.at[half, 1, step],
                    target,
                )
                self.second[half, step].start()

    def finish(self):
        _, y, x = place()
        totals = []
        for half in range(2):
            for step in STEPS:
                self.second[half, step].wait_recv()
            total = self.mid[half, (y, x)[half]].astype(F32)
            for step in STEPS:
                total += self.last[half, step - 1].astype(F32)
            totals.append(total)
        return totals

    def drain(self):
        for copy in [*self.first.values(), *self.second.values()]:
            copy.wait_send()


def table_kernel(parents, slots, where_to):
    me, _, _ = place()
    for t in range(2):
        cur = parents[2 * me + t]
        for i in range(DEPTH):
            slots[t, i] = jnp.where(cur >= 0, cur, SEGS)
            cur = jnp.where(cur >= 0, parents[jnp.maximum(cur, 0)], -1)

    def find(j):
        for t in range(2):
            found = jnp.where(j == 2 * me + t, DEPTH, SLOTS)
            for i in range(DEPTH):
                found = jnp.where(slots[t, i] == j, i, found)
            where_to[t, j] = found

    loop(SEGS, find)


def kernel(
    hid_ref, q_ref, k_ref, v_ref, g_ref, slots, where_to,
    dq_ref, proj_ref,
    hid, hid_t, q, g, k_all, v_all, kc, vc, kct, vct, qt, gt, qs, gs,
    e, p, mxs, inv, delta, dva, dka, low,
    kv_stage, kv_got, kv_mid, kv_last, pr_stage, pr_got, pr_mid, pr_last,
    local_sem, gather_send, gather_recv, sum_send, sum_recv,
):
    me, y, x = place()
    locals_ = [
        pltpu.make_async_copy(src, dst, local_sem.at[i])
        for i, (src, dst) in enumerate(((q_ref, q), (g_ref, g), (hid_ref, hid)))
    ]
    for copy in locals_:
        copy.start()

    barrier = pltpu.get_barrier_semaphore()
    for step in STEPS:
        for mate in (at(0, step), at(step, 0)):
            pl.semaphore_signal(barrier, inc=1, device_id={"seq": mate}, device_id_type=MESH)
    for half in range(2):
        k_all[2 * me + half] = k_ref[half * SEG : (half + 1) * SEG, :]
        v_all[2 * me + half] = v_ref[half * SEG : (half + 1) * SEG, :]
    pl.semaphore_wait(barrier, 6)

    keys = Gather(k_all, gather_send.at[0], gather_recv.at[0])
    vals = Gather(v_all, gather_send.at[1], gather_recv.at[1])
    keys.own()
    vals.own()

    locals_[0].wait()
    locals_[1].wait()

    def prepare(u):
        t = u // PAIRS
        first = lax.rem(u, PAIRS) * W
        rows = pl.ds(pl.multiple_of(t * SEG, SEG), SEG)
        for src, turned, stacked in ((q, qt, qs), (g, gt, gs)):
            for k in range(2):
                block = src[rows, pl.ds(pl.multiple_of(first + k * HD, HD), HD)]
                stacked[u, pl.ds(k * SEG, SEG), :] = block
                turned[u, :, pl.ds(k * SEG, SEG)] = block.T

    loop(UNITS, prepare)
    keys.forward()
    vals.forward()

    locals_[2].wait()

    def turn(c):
        cols = pl.ds(pl.multiple_of(c * HD, HD), HD)
        hid_t[cols, :] = hid[:, cols].T

    loop(D // HD, turn)

    def collect(source, rows_out, cols_out):
        for t in range(2):
            if source is k_all:
                head = source[2 * me + t, 0:16, :].astype(F32)[0:1]
                source[SEGS] = jnp.broadcast_to(head, (SEG, HD)).astype(BF)
            for i in range(SLOTS):
                block = source[slots[t, i]] if i < DEPTH else source[2 * me + t]
                rows_out[t, pl.ds(i * SEG, SEG), :] = block
                cols_out[t, :, pl.ds(i * SEG, SEG)] = block.T

    keys.arrive()
    collect(k_all, kc, kct)
    loop(UNITS, lambda u: score_unit(u, kc, qt, e, mxs))
    loop(UNITS, lambda u: prob_unit(u, slots, e, mxs, inv, p))

    vals.arrive()
    v_all[SEGS] = jnp.zeros((SEG, HD), BF)
    collect(v_all, vc, vct)
    loop(UNITS, lambda u: delta_unit(u, vct, gt, p, delta))

    def spread(acc, reduce):
        def put(dest):
            blocks = []
            for half in range(2):
                block = jnp.zeros((SEG, HD), F32)
                for t in range(2):
                    block += acc[t, where_to[t, 2 * dest + half]]
                blocks.append(block)
            reduce.put(dest, *blocks)

        loop(RANKS, put)
        reduce.start()

    def make(i, stage, got, mid, last):
        j = i % 2
        return Reduce(
            stage.at[j], got.at[j], mid.at[j], last.at[j], sum_send.at[i], sum_recv.at[i]
        )

    dv = make(0, kv_stage, kv_got, kv_mid, kv_last)
    dk = make(1, kv_stage, kv_got, kv_mid, kv_last)
    pv = make(2, pr_stage, pr_got, pr_mid, pr_last)
    pk = make(3, pr_stage, pr_got, pr_mid, pr_last)

    def project(reduce, grad, scale):
        for half, total in enumerate(grad.finish()):
            low[pl.ds(half * SEG, SEG), :] = (total * scale).astype(BF)
        weights = low[...]

        def put(dest):
            rows = pl.ds(pl.multiple_of(dest * DCOLS, 64), DCOLS)
            out = dot(hid_t[rows, :], weights)
            reduce.put(dest, out[: DCOLS // 2], out[DCOLS // 2 :])

        loop(RANKS, put)
        reduce.start()

    for t in range(2):
        side_grad(t, p, gs, dva)
    spread(dva, dv)
    loop(UNITS, lambda u: ds_unit(u, vc, gt, e, inv, delta, p))
    dv.middle()
    for t in range(2):
        side_grad(t, p, qs, dka)
    spread(dka, dk)
    project(pv, dv, 1.0)
    loop(UNITS, lambda u: dq_unit(u, kct, p, dq_ref))
    dk.middle()
    pv.middle()
    project(pk, dk, SCALE)
    pk.middle()
    for half, total in enumerate(pv.finish()):
        proj_ref[pl.ds(half * (DCOLS // 2), DCOLS // 2), pl.ds(HD, HD)] = total
    for half, total in enumerate(pk.finish()):
        proj_ref[pl.ds(half * (DCOLS // 2), DCOLS // 2), pl.ds(0, HD)] = total
    for part in (keys, vals, dv, dk, pv, pk):
        part.drain()


def on_device(hidden_in, queries, keys, values, out_grad, parents):
    vmem = pl.BlockSpec(memory_space=pltpu.VMEM)
    hbm = pl.BlockSpec(memory_space=pl.ANY)
    smem = pl.BlockSpec(memory_space=pltpu.SMEM)
    tokens = 2 * SEG
    half = DCOLS // 2
    scratch = [
        pltpu.VMEM((tokens, D), BF),
        pltpu.VMEM((D, tokens), BF),
        pltpu.VMEM((tokens, GROUP * HD), BF),
        pltpu.VMEM((tokens, GROUP * HD), BF),
        pltpu.VMEM((SEGS + 1, SEG, HD), BF),
        pltpu.VMEM((SEGS + 1, SEG, HD), BF),
        pltpu.VMEM((2, KEYS, HD), BF),
        pltpu.VMEM((2, KEYS, HD), BF),
        pltpu.VMEM((2, HD, KEYS), BF),
        pltpu.VMEM((2, HD, KEYS), BF),
        pltpu.VMEM((UNITS, HD, W), BF),
        pltpu.VMEM((UNITS, HD, W), BF),
        pltpu.VMEM((UNITS, W, HD), BF),
        pltpu.VMEM((UNITS, W, HD), BF),
        pltpu.VMEM((UNITS, KEYS, W), F32),
        pltpu.VMEM((UNITS, KEYS, W), BF),
        pltpu.VMEM((UNITS, 8, W), F32),
        pltpu.VMEM((UNITS, 8, W), F32),
        pltpu.VMEM((UNITS, 8, W), F32),
        pltpu.VMEM((2, SLOTS + 1, SEG, HD), F32),
        pltpu.VMEM((2, SLOTS + 1, SEG, HD), F32),
        pltpu.VMEM((tokens, HD), BF),
        pltpu.VMEM((2, 2, SIDE, SIDE, SEG, HD), BF),
        pltpu.VMEM((2, 2, 3, SIDE, SEG, HD), BF),
        pltpu.VMEM((2, 2, SIDE, SEG, HD), BF),
        pltpu.VMEM((2, 2, 3, SEG, HD), BF),
        pltpu.VMEM((2, 2, SIDE, SIDE, half, HD), BF),
        pltpu.VMEM((2, 2, 3, SIDE, half, HD), BF),
        pltpu.VMEM((2, 2, SIDE, half, HD), BF),
        pltpu.VMEM((2, 2, 3, half, HD), BF),
        pltpu.SemaphoreType.DMA((3,)),
        pltpu.SemaphoreType.DMA((2, 2, RANKS)),
        pltpu.SemaphoreType.DMA((2, 2, RANKS)),
        pltpu.SemaphoreType.DMA((4, 2, 2, SIDE)),
        pltpu.SemaphoreType.DMA((4, 2, 2, SIDE)),
    ]
    slots, where_to = pl.pallas_call(
        table_kernel,
        out_shape=(
            jax.ShapeDtypeStruct((2, DEPTH), jnp.int32),
            jax.ShapeDtypeStruct((2, SEGS), jnp.int32),
        ),
        in_specs=[smem],
        out_specs=(smem, smem),
    )(parents)
    return pl.pallas_call(
        kernel,
        out_shape=(
            jax.ShapeDtypeStruct((tokens, GROUP * HD), BF),
            jax.ShapeDtypeStruct((DCOLS, 2 * HD), F32),
        ),
        in_specs=[hbm, hbm, vmem, vmem, hbm, smem, smem],
        out_specs=(vmem, vmem),
        scratch_shapes=scratch,
        compiler_params=pltpu.CompilerParams(
            collective_id=1, has_side_effects=True, vmem_limit_bytes=60 << 20
        ),
    )(hidden_in, queries, keys, values, out_grad, slots, where_to)


def solution(mesh):
    rows = P(("leaf", "seq"), None)
    return jax.shard_map(
        on_device,
        mesh=mesh,
        in_specs=(rows, rows, rows, rows, rows, P("leaf")),
        out_specs=(rows, rows),
        check_vma=False,
    )
```

time: 388 us -> 82.5 us (0.21)
  waiting for transfers between devices: 217 us -> 0 us
  matrix products: 83.1 us -> 0 us
  Pallas kernels: 0 us -> 78 us
  local copies, waits for them, and re-layouts: 49.9 us -> 3.59 us
  other arithmetic: 18.6 us -> 0 us
  between operations: 13.9 us -> 0.65 us
    dot_general x35 -> x0, matrix products: 83.1 us -> none  [the longest x4 20.5 us: output_live(): jnp.einsum('gqk,kd->qgd', probs.astype(jnp.bfloat16), value_rows, preferr...]
    pallas_call x0 -> x2, Pallas kernels: none -> 78 us  [the longest x1 75.6 us: on_device(): pl.pallas_call(kernel, out_shape=(jax.ShapeDtypeStruct((tokens, GROUP * H...]
    unnamed x5 -> x0, waiting for transfers between devices: 77.4 us -> none
    reduce_scatter x1 -> x0, waiting for transfers between devices: 76.9 us -> none  [on_device(): kv_grad = lax.psum_scatter(result, 'seq', scatter_dimension=0, tiled=True)]
    all_gather x2 -> x0, waiting for transfers between devices: 63.1 us -> none  [the longest x1 40.4 us: on_device(): lax.all_gather(keys, 'seq', axis=0, tiled=True)]
    dynamic_update_slice x8 -> x0, local copies, waits for them, and re-layouts: 19.4 us -> none  [on_device(): lax.scan(grad_step, jnp.zeros((local_len, group, head_width), jnp.float32...]
    or x12 -> x0, local copies, waits for them, and re-layouts: 10.2 us -> none  [pair_mask(): return coarse | same_seg & (key_pos[None, :] <= query_pos[:, None])]
    reduce_sum x5 -> x0, other arithmetic: 8.34 us -> none  [the longest x4 6.86 us: stat_live(): jnp.sum(jnp.exp(scores - new_max[..., None]), axis=-1)]
  transfers between devices with their start and end apart: 4 -> 0, of which waited for: 4 -> 0; matrix products, arithmetic and copies ran while one was open for 8% -> 0% of each run, Pallas kernels for 0% -> 0%
where the time goes in v1:
time: 82.5 us; the launch traced here: 82.3 us
  Pallas kernels  78 us (95%)
  local copies, waits for them, and re-layouts  3.59 us (4%)
    pallas_call x1, Pallas kernels, on_device(): pl.pallas_call(kernel, out_shape=(jax.ShapeDtypeStruct((tokens, GROUP * H...  75.6 us
    unnamed x2, local copies, waits for them, and re-layouts  3.59 us
    pallas_call x1, Pallas kernels, on_device(): pl.pallas_call(table_kernel, out_shape=(jax.ShapeDtypeStruct((2, DEPTH),...  2.46 us

profile of v1, /device:TPU:0, one launch (start us, length us, event | category | flops | bytes accessed | tf_op | source)
XLA Modules:
  0.0 82.3 jit_solution(2083210494896824300)
XLA Ops:
  0.6 2.5 %shard_map.77 = (s32[2,16]{1,0:T(2,128)}, s32[2,32]{1,0:T(2,128)}) custom-call(s32[32]{0:T(128)} %parents.1), custom_call_target="tpu_custom_call" | custom-call | tf_op jit(solution)/shard_map/pallas_call | solution.py:433
  3.1 75.6 %shard_map.78 = (bf16[256,1024]{1,0:T(8,128)(2,1)}, f32[320,256]{1,0:T(8,128)}) custom-call(bf16[256,5120]{1,0:T(8,128)(2,1)} %hid_ref.1, bf16[256,1024]{1,0:T(8,128)(2,1)} %q_ref.1, bf16[256,128]{1,0:T(8,128)(2,1)} %k_ref.1, bf16[256,128]{1,0:T(8,128)(2,1)} %v_ref.1, bf16[256,1024]{1,0:T(8,128)(2,1)} %g_ref.1, s32[2,16]{1,0:T(2,128)} %get-tuple-element.4.slots, ...), custom_call_target="tpu_custom_call" | custom-call | tf_op jit(solution)/shard_map/pallas_call | solution.py:442
  78.7 1.9 %copy.10 = bf16[256,1024]{1,0:T(8,128)(2,1)} copy(bf16[256,1024]{1,0:T(8,128)(2,1)} %get-tuple-element.8) | data formatting | bytes 1048576
  80.5 1.7 %copy.11 = f32[320,256]{1,0:T(8,128)} copy(f32[320,256]{1,0:T(8,128)} %get-tuple-element.9) | data formatting | bytes 655360

commit v2 on v1

--- a/solution.py
+++ b/solution.py
@@ -56,46 +56,102 @@
     lax.fori_loop(0, count, step, 0)
 
 
-def score_unit(u, kc, qt, e, mxs):
-    t = u // PAIRS
+def interleave(*parts):
+    timed = [((i + 0.5) / len(part), n, i) for n, part in enumerate(parts) for i in range(len(part))]
+    for _, n, i in sorted(timed):
+        parts[n][i]()
+
+
+def paired(first, second):
+    interleave(first((0, 0)))
+
+    def body(i):
+        interleave(first((1, i)), second((0, i)))
+        interleave(first((0, i + 1)), second((1, i)))
+
+    loop(UNITS // 2 - 1, body)
+    end = UNITS // 2 - 1
+    interleave(first((1, end)), second((0, end)))
+    interleave(second((1, end)))
+
+
+def score_steps(unit, kc, qt, e, mxs):
+    parity, index = unit
+    u, t = 2 * index + parity, index // 2
     weights = qt[u]
-    key = lax.broadcasted_iota(jnp.int32, (SEG, W), 0)
-    row = lax.broadcasted_iota(jnp.int32, (SEG, W), 1)
-    row = jnp.where(row >= SEG, row - SEG, row)
-    mx = jnp.full((8, W), -3e38, F32)
-    for start in range(0, KEYS, MC):
+    state = [jnp.full((8, W), -3e38, F32)]
+
+    def step(start):
         s = dot(kc[t, pl.ds(start, MC), :], weights)
         if start + MC == KEYS:
+            key = lax.broadcasted_iota(jnp.int32, (SEG, W), 0)
+            row = lax.broadcasted_iota(jnp.int32, (SEG, W), 1)
+            row = jnp.where(row >= SEG, row - SEG, row)
             own = jnp.where(key <= row, s[MC - SEG :], -PEN)
             s = jnp.concatenate([s[: MC - SEG], own], axis=0)
-        e[u, pl.ds(start, MC), :] = s
-        mx = jnp.maximum(mx, jnp.max(s.reshape(MC // 8, 8, W), axis=0))
-    mxs[u] = mx
-
-
-def prob_unit(u, slots, e, mxs, inv, p):
-    t = u // PAIRS
+        e[parity][index, pl.ds(start, MC), :] = s
+        state[0] = jnp.maximum(state[0], jnp.max(s.reshape(MC // 8, 8, W), axis=0))
+        if start + MC == KEYS:
+            mxs[u] = state[0]
+
+    return [functools.partial(step, start) for start in range(0, KEYS, MC)]
+
+
+def prob_steps(unit, slots, e, mxs, inv, p):
+    parity, index = unit
+    u, t = 2 * index + parity, index // 2
     m = jnp.max(mxs[u], axis=0, keepdims=True) * (SCALE * LOG2E)
-    acc = jnp.zeros((8, W), F32)
-    for i in range(SLOTS):
+    state = [jnp.zeros((8, W), F32), None]
+
+    def power(i):
         rows = pl.ds(i * SEG, SEG)
         shift = m
         if i < DEPTH:
             shift = m + jnp.where(slots[t, i] == SEGS, jnp.float32(PEN), jnp.float32(0.0))
-        x = jnp.exp2(e[u, rows, :] * (SCALE * LOG2E) - shift)
-        e[u, rows, :] = x
-        acc = acc + jnp.sum(x.reshape(SEG // 8, 8, W), axis=0)
-    r = 1.0 / jnp.sum(acc, axis=0, keepdims=True)
-    inv[u] = jnp.broadcast_to(r, (8, W))
-    for i in range(SLOTS):
+        x = jnp.exp2(e[parity][index, rows, :] * (SCALE * LOG2E) - shift)
+        e[parity][index, rows, :] = x
+        state[0] += jnp.sum(x.reshape(SEG // 8, 8, W), axis=0)
+
+    def norm(i):
         rows = pl.ds(i * SEG, SEG)
-        p[u, rows, :] = (e[u, rows, :] * r).astype(BF)
-
-
-def delta_unit(u, vct, gt, p, delta):
-    o = dot(vct[u // PAIRS], p[u])
-    d = jnp.sum(gt[u].astype(F32) * o, axis=0, keepdims=True)
-    delta[u] = jnp.broadcast_to(d, (8, W))
+        if i == 0:
+            state[1] = 1.0 / jnp.sum(state[0], axis=0, keepdims=True)
+            inv[u] = jnp.broadcast_to(state[1], (8, W))
+        p[u, rows, :] = (e[parity][index, rows, :] * state[1]).astype(BF)
+
+    return [functools.partial(f, i) for f in (power, norm) for i in range(SLOTS)]
+
+
+def dprob_steps(unit, vc, gt, e, inv, dp, delta):
+    parity, index = unit
+    u, t = 2 * index + parity, index // 2
+    weights = gt[u]
+    state = [jnp.zeros((8, W), F32)]
+
+    def step(start):
+        rows = pl.ds(start, MC)
+        x = dot(vc[t, rows, :], weights)
+        dp[parity][rows, :] = x
+        x = x * e[parity][index, rows, :]
+        state[0] += jnp.sum(x.reshape(MC // 8, 8, W), axis=0)
+        if start + MC == KEYS:
+            total = jnp.sum(state[0], axis=0, keepdims=True) * inv[u, 0:1, :]
+            delta[u] = jnp.broadcast_to(total, (8, W))
+
+    return [functools.partial(step, start) for start in range(0, KEYS, MC)]
+
+
+def dscore_steps(unit, e, inv, dp, delta, ds):
+    parity, index = unit
+    u = 2 * index + parity
+    r = inv[u, 0:1, :]
+    d = delta[u, 0:1, :]
+
+    def step(i):
+        rows = pl.ds(i * SEG, SEG)
+        ds[u, rows, :] = (e[parity][index, rows, :] * r * (dp[parity][rows, :] - d)).astype(BF)
+
+    return [functools.partial(step, i) for i in range(SLOTS)]
 
 
 def side_grad(t, lhs, rhs, acc):
@@ -104,17 +160,6 @@
         total += dot(lhs[t * PAIRS + h], rhs[t * PAIRS + h])
     acc[t, pl.ds(0, SLOTS)] = total.reshape(SLOTS, SEG, HD)
     acc[t, SLOTS] = jnp.zeros((SEG, HD), F32)
-
-
-def ds_unit(u, vc, gt, e, inv, delta, ds):
-    t = u // PAIRS
-    weights = gt[u]
-    r = inv[u, 0:1, :]
-    d = delta[u, 0:1, :]
-    for start in range(0, KEYS, MC):
-        rows = pl.ds(start, MC)
-        dp = dot(vc[t, rows, :], weights)
-        ds[u, rows, :] = (e[u, rows, :] * r * (dp - d)).astype(BF)
 
 
 def dq_unit(u, kct, ds, dq):
@@ -256,15 +301,19 @@
 def kernel(
     hid_ref, q_ref, k_ref, v_ref, g_ref, slots, where_to,
     dq_ref, proj_ref,
-    hid, hid_t, q, g, k_all, v_all, kc, vc, kct, vct, qt, gt, qs, gs,
-    e, p, mxs, inv, delta, dva, dka, low,
+    hid_t, q, g, k_all, v_all, kc, vc, kct, qt, gt, qs, gs,
+    e0, e1, dp0, dp1, p, mxs, inv, delta, side, low,
     kv_stage, kv_got, kv_mid, kv_last, pr_stage, pr_got, pr_mid, pr_last,
     local_sem, gather_send, gather_recv, sum_send, sum_recv,
 ):
     me, y, x = place()
+    def park(c):
+        return p.at[c % UNITS, pl.ds(c // UNITS * W, W), :]
+
+    moves = [(q_ref, q), (g_ref, g)]
+    moves += [(hid_ref.at[:, pl.ds(c * W, W)], park(c)) for c in range(D // W)]
     locals_ = [
-        pltpu.make_async_copy(src, dst, local_sem.at[i])
-        for i, (src, dst) in enumerate(((q_ref, q), (g_ref, g), (hid_ref, hid)))
+        pltpu.make_async_copy(src, dst, local_sem.at[i]) for i, (src, dst) in enumerate(moves)
     ]
     for copy in locals_:
         copy.start()
@@ -281,7 +330,6 @@
     keys = Gather(k_all, gather_send.at[0], gather_recv.at[0])
     vals = Gather(v_all, gather_send.at[1], gather_recv.at[1])
     keys.own()
-    vals.own()
 
     locals_[0].wait()
     locals_[1].wait()
@@ -298,35 +346,26 @@
 
     loop(UNITS, prepare)
     keys.forward()
+    vals.own()
     vals.forward()
 
-    locals_[2].wait()
-
-    def turn(c):
-        cols = pl.ds(pl.multiple_of(c * HD, HD), HD)
-        hid_t[cols, :] = hid[:, cols].T
-
-    loop(D // HD, turn)
-
-    def collect(source, rows_out, cols_out):
-        for t in range(2):
-            if source is k_all:
-                head = source[2 * me + t, 0:16, :].astype(F32)[0:1]
-                source[SEGS] = jnp.broadcast_to(head, (SEG, HD)).astype(BF)
-            for i in range(SLOTS):
-                block = source[slots[t, i]] if i < DEPTH else source[2 * me + t]
-                rows_out[t, pl.ds(i * SEG, SEG), :] = block
-                cols_out[t, :, pl.ds(i * SEG, SEG)] = block.T
-
+    for c in range(D // W):
+        locals_[2 + c].wait()
+        hid_t[pl.ds(c * W, W), :] = park(c)[...].T
+
+    e, dp = (e0, e1), (dp0, dp1)
     keys.arrive()
-    collect(k_all, kc, kct)
-    loop(UNITS, lambda u: score_unit(u, kc, qt, e, mxs))
-    loop(UNITS, lambda u: prob_unit(u, slots, e, mxs, inv, p))
-
-    vals.arrive()
-    v_all[SEGS] = jnp.zeros((SEG, HD), BF)
-    collect(v_all, vc, vct)
-    loop(UNITS, lambda u: delta_unit(u, vct, gt, p, delta))
+    for t in range(2):
+        head = k_all[2 * me + t, 0:16, :].astype(F32)[0:1]
+        k_all[SEGS] = jnp.broadcast_to(head, (SEG, HD)).astype(BF)
+        for i in range(SLOTS):
+            block = k_all[slots[t, i]] if i < DEPTH else k_all[2 * me + t]
+            kc[t, pl.ds(i * SEG, SEG), :] = block
+            kct[t, :, pl.ds(i * SEG, SEG)] = block.T
+    paired(
+        lambda unit: score_steps(unit, kc, qt, e, mxs),
+        lambda unit: prob_steps(unit, slots, e, mxs, inv, p),
+    )
 
     def spread(acc, reduce):
         def put(dest):
@@ -363,21 +402,32 @@
             reduce.put(dest, out[: DCOLS // 2], out[DCOLS // 2 :])
 
         loop(RANKS, put)
-        reduce.start()
 
     for t in range(2):
-        side_grad(t, p, gs, dva)
-    spread(dva, dv)
-    loop(UNITS, lambda u: ds_unit(u, vc, gt, e, inv, delta, p))
+        side_grad(t, p, gs, side)
+    spread(side, dv)
+
+    vals.arrive()
+    v_all[SEGS] = jnp.zeros((SEG, HD), BF)
+    for t in range(2):
+        for i in range(SLOTS):
+            block = v_all[slots[t, i]] if i < DEPTH else v_all[2 * me + t]
+            vc[t, pl.ds(i * SEG, SEG), :] = block
+    paired(
+        lambda unit: dprob_steps(unit, vc, gt, e, inv, dp, delta),
+        lambda unit: dscore_steps(unit, e, inv, dp, delta, p),
+    )
     dv.middle()
     for t in range(2):
-        side_grad(t, p, qs, dka)
-    spread(dka, dk)
+        side_grad(t, p, qs, side)
+    spread(side, dk)
+    loop(UNITS, lambda u: dq_unit(u, kct, p, dq_ref))
     project(pv, dv, 1.0)
-    loop(UNITS, lambda u: dq_unit(u, kct, p, dq_ref))
     dk.middle()
+    pv.start()
+    project(pk, dk, SCALE)
+    pk.start()
     pv.middle()
-    project(pk, dk, SCALE)
     pk.middle()
     for half, total in enumerate(pv.finish()):
         proj_ref[pl.ds(half * (DCOLS // 2), DCOLS // 2), pl.ds(HD, HD)] = total
@@ -387,6 +437,11 @@
         part.drain()
 
 
+def copy_kernel(dq_in, proj_in, dq_out, proj_out):
+    dq_out[...] = dq_in[...]
+    proj_out[...] = proj_in[...]
+
+
 def on_device(hidden_in, queries, keys, values, out_grad, parents):
     vmem = pl.BlockSpec(memory_space=pltpu.VMEM)
     hbm = pl.BlockSpec(memory_space=pl.ANY)
@@ -394,7 +449,6 @@
     tokens = 2 * SEG
     half = DCOLS // 2
     scratch = [
-        pltpu.VMEM((tokens, D), BF),
         pltpu.VMEM((D, tokens), BF),
         pltpu.VMEM((tokens, GROUP * HD), BF),
         pltpu.VMEM((tokens, GROUP * HD), BF),
@@ -403,17 +457,18 @@
         pltpu.VMEM((2, KEYS, HD), BF),
         pltpu.VMEM((2, KEYS, HD), BF),
         pltpu.VMEM((2, HD, KEYS), BF),
-        pltpu.VMEM((2, HD, KEYS), BF),
         pltpu.VMEM((UNITS, HD, W), BF),
         pltpu.VMEM((UNITS, HD, W), BF),
         pltpu.VMEM((UNITS, W, HD), BF),
         pltpu.VMEM((UNITS, W, HD), BF),
-        pltpu.VMEM((UNITS, KEYS, W), F32),
+        pltpu.VMEM((UNITS // 2, KEYS, W), F32),
+        pltpu.VMEM((UNITS // 2, KEYS, W), F32),
+        pltpu.VMEM((KEYS, W), F32),
+        pltpu.VMEM((KEYS, W), F32),
         pltpu.VMEM((UNITS, KEYS, W), BF),
         pltpu.VMEM((UNITS, 8, W), F32),
         pltpu.VMEM((UNITS, 8, W), F32),
         pltpu.VMEM((UNITS, 8, W), F32),
-        pltpu.VMEM((2, SLOTS + 1, SEG, HD), F32),
         pltpu.VMEM((2, SLOTS + 1, SEG, HD), F32),
         pltpu.VMEM((tokens, HD), BF),
         pltpu.VMEM((2, 2, SIDE, SIDE, SEG, HD), BF),
@@ -424,7 +479,7 @@
         pltpu.VMEM((2, 2, 3, SIDE, half, HD), BF),
         pltpu.VMEM((2, 2, SIDE, half, HD), BF),
         pltpu.VMEM((2, 2, 3, half, HD), BF),
-        pltpu.SemaphoreType.DMA((3,)),
+        pltpu.SemaphoreType.DMA((2 + D // W,)),
         pltpu.SemaphoreType.DMA((2, 2, RANKS)),
         pltpu.SemaphoreType.DMA((2, 2, RANKS)),
         pltpu.SemaphoreType.DMA((4, 2, 2, SIDE)),
@@ -439,19 +494,26 @@
         in_specs=[smem],
         out_specs=(smem, smem),
     )(parents)
-    return pl.pallas_call(
+    out_shape = (
+        jax.ShapeDtypeStruct((tokens, GROUP * HD), BF),
+        jax.ShapeDtypeStruct((DCOLS, 2 * HD), F32),
+    )
+    grads = pl.pallas_call(
         kernel,
-        out_shape=(
-            jax.ShapeDtypeStruct((tokens, GROUP * HD), BF),
-            jax.ShapeDtypeStruct((DCOLS, 2 * HD), F32),
-        ),
+        out_shape=out_shape,
         in_specs=[hbm, hbm, vmem, vmem, hbm, smem, smem],
         out_specs=(vmem, vmem),
         scratch_shapes=scratch,
         compiler_params=pltpu.CompilerParams(
-            collective_id=1, has_side_effects=True, vmem_limit_bytes=60 << 20
+            collective_id=1, has_side_effects=True, vmem_limit_bytes=62 << 20
         ),
     )(hidden_in, queries, keys, values, out_grad, slots, where_to)
+    return pl.pallas_call(
+        copy_kernel,
+        out_shape=out_shape,
+        in_specs=[vmem, vmem],
+        out_specs=(vmem, vmem),
+    )(*grads)
 
 
 def solution(mesh):

time: 82.5 us -> 76 us (0.921)
  local copies, waits for them, and re-layouts: 3.59 us -> 0 us
  Pallas kernels: 78 us -> 75.2 us
    unnamed x2 -> x0, local copies, waits for them, and re-layouts: 3.59 us -> none
    pallas_call x1 -> x2, Pallas kernels: 75.6 us -> 72.7 us  [the longest x1 70.7 us: on_device(): pl.pallas_call(kernel, out_shape=out_shape, in_specs=[hbm, hbm, vmem, vme...]
where the time goes in v2:
time: 76 us; the launch traced here: 75.8 us
  Pallas kernels  75.2 us (99%)
    pallas_call x1, Pallas kernels, on_device(): pl.pallas_call(kernel, out_shape=out_shape, in_specs=[hbm, hbm, vmem, vme...  70.7 us
    pallas_call x1, Pallas kernels, on_device(): pl.pallas_call(table_kernel, out_shape=(jax.ShapeDtypeStruct((2, DEPTH),...  2.46 us
    pallas_call x1, Pallas kernels, on_device(): pl.pallas_call(copy_kernel, out_shape=out_shape, in_specs=[vmem, vmem], o...  2.06 us

profile of v2, /device:TPU:0, one launch (start us, length us, event | category | flops | bytes accessed | tf_op | source)
XLA Modules:
  0.0 75.8 jit_solution(2272382680027779516)
XLA Ops:
  0.6 2.5 %shard_map.77 = (s32[2,16]{1,0:T(2,128)}, s32[2,32]{1,0:T(2,128)}) custom-call(s32[32]{0:T(128)} %parents.1), custom_call_target="tpu_custom_call" | custom-call | tf_op jit(solution)/shard_map/pallas_call | solution.py:488
  3.1 70.7 %shard_map.78 = (bf16[256,1024]{1,0:T(8,128)(2,1)}, f32[320,256]{1,0:T(8,128)}) custom-call(bf16[256,5120]{1,0:T(8,128)(2,1)} %hid_ref.1, bf16[256,1024]{1,0:T(8,128)(2,1)} %q_ref.1, bf16[256,128]{1,0:T(8,128)(2,1)} %k_ref.1, bf16[256,128]{1,0:T(8,128)(2,1)} %v_ref.1, bf16[256,1024]{1,0:T(8,128)(2,1)} %g_ref.1, s32[2,16]{1,0:T(2,128)} %get-tuple-element.6.slots, ...), custom_call_target="tpu_custom_call" | custom-call | tf_op jit(solution)/shard_map/pallas_call | solution.py:501
  73.8 2.1 %shard_map.79 = (bf16[256,1024]{1,0:T(8,128)(2,1)}, f32[320,256]{1,0:T(8,128)}) custom-call(bf16[256,1024]{1,0:T(8,128)(2,1)} %get-tuple-element.8.dq_in, f32[320,256]{1,0:T(8,128)} %get-tuple-element.9.proj_in), custom_call_target="tpu_custom_call" | custom-call | tf_op jit(solution)/shard_map/pallas_call | solution.py:511

commit v3 on v2

--- a/solution.py
+++ b/solution.py
@@ -215,96 +215,85 @@
 
 
 class Reduce:
-    def __init__(self, stage, got, mid, last, send, recv):
-        self.stage, self.got, self.mid, self.last = stage, got, mid, last
-        self.send, self.recv = send, recv
+    def __init__(self, stage, own, got, mid, last, send, recv, send_on, recv_on):
+        self.stage, self.own, self.got, self.mid, self.last = stage, own, got, mid, last
+        self.send, self.recv, self.send_on, self.recv_on = send, recv, send_on, recv_on
         self.first, self.second = {}, {}
 
-    def put(self, dest, low, high):
-        y, x = dest // SIDE, lax.rem(dest, SIDE)
-        self.stage[0, x, y] = low.astype(BF)
-        self.stage[1, y, x] = high.astype(BF)
+    def scatter(self, block, now=True):
+        _, y, x = place()
+        for step in (*STEPS, 0):
+            for half in range(2):
+                mine, other = ((x, y), (y, x))[half]
+                column = lax.rem(mine + step, SIDE)
+                for j in range(SIDE):
+                    k = lax.rem(other + 1 + j, SIDE)
+                    rank = k * SIDE + column if half == 0 else column * SIDE + k
+                    value = block(rank, half)
+                    if step == 0:
+                        self.own[half, k] = value
+                        continue
+                    self.stage[half, step - 1, k] = value.astype(BF)
+                    copy = remote(
+                        self.stage.at[half, step - 1, k],
+                        self.got.at[half, step - 1, k],
+                        self.send.at[half, step, j],
+                        self.recv.at[half, step, j],
+                        (at(0, step), at(step, 0))[half],
+                    )
+                    self.first[half, step, j] = copy
+                    if now:
+                        copy.start()
 
     def start(self):
-        _, y, x = place()
-        for step in STEPS:
-            for half in range(2):
-                column = lax.rem((x, y)[half] + step, SIDE)
-                target = (at(0, step), at(step, 0))[half]
-                self.first[half, step] = remote(
-                    self.stage.at[half, column],
-                    self.got.at[half, step - 1],
-                    self.send.at[half, 0, step],
-                    self.recv.at[half, 0, step],
-                    target,
-                )
-                self.first[half, step].start()
+        for copy in self.first.values():
+            copy.start()
 
     def middle(self):
         _, y, x = place()
-        for half in range(2):
-            for step in STEPS:
-                self.first[half, step].wait_recv()
-            here = (x, y)[half]
-            for k in range(SIDE):
-                total = self.stage[half, here, k].astype(F32)
+        for j in range(SIDE):
+            for half in range(2):
+                k = lax.rem((y, x)[half] + 1 + j, SIDE)
+                for step in STEPS:
+                    self.first[half, step, j].wait_recv()
+                total = self.own[half, k]
                 for step in STEPS:
                     total += self.got[half, step - 1, k].astype(F32)
-                self.mid[half, k] = total.astype(BF)
-            for step in STEPS:
-                row = lax.rem((y, x)[half] + step, SIDE)
-                target = (at(step, 0), at(0, step))[half]
-                self.second[half, step] = remote(
-                    self.mid.at[half, row],
-                    self.last.at[half, step - 1],
-                    self.send.at[half, 1, step],
-                    self.recv.at[half, 1, step],
-                    target,
+                if j == SIDE - 1:
+                    self.own[half, k] = total
+                    continue
+                self.mid[half, j] = total.astype(BF)
+                copy = remote(
+                    self.mid.at[half, j],
+                    self.last.at[half, j],
+                    self.send_on.at[half, j],
+                    self.recv_on.at[half, j],
+                    (at(j + 1, 0), at(0, j + 1))[half],
                 )
-                self.second[half, step].start()
-
-    def finish(self):
+                copy.start()
+                self.second[half, j] = copy
+
+    def finish(self, half):
         _, y, x = place()
-        totals = []
-        for half in range(2):
-            for step in STEPS:
-                self.second[half, step].wait_recv()
-            total = self.mid[half, (y, x)[half]].astype(F32)
-            for step in STEPS:
-                total += self.last[half, step - 1].astype(F32)
-            totals.append(total)
-        return totals
+        total = self.own[half, (y, x)[half]]
+        for j in range(SIDE - 1):
+            self.second[half, j].wait_recv()
+            total += self.last[half, j].astype(F32)
+        return total
 
     def drain(self):
         for copy in [*self.first.values(), *self.second.values()]:
             copy.wait_send()
 
 
-def table_kernel(parents, slots, where_to):
-    me, _, _ = place()
-    for t in range(2):
-        cur = parents[2 * me + t]
-        for i in range(DEPTH):
-            slots[t, i] = jnp.where(cur >= 0, cur, SEGS)
-            cur = jnp.where(cur >= 0, parents[jnp.maximum(cur, 0)], -1)
-
-    def find(j):
-        for t in range(2):
-            found = jnp.where(j == 2 * me + t, DEPTH, SLOTS)
-            for i in range(DEPTH):
-                found = jnp.where(slots[t, i] == j, i, found)
-            where_to[t, j] = found
-
-    loop(SEGS, find)
-
-
 def kernel(
-    hid_ref, q_ref, k_ref, v_ref, g_ref, slots, where_to,
+    hid_ref, q_ref, k_ref, v_ref, g_ref, parents,
     dq_ref, proj_ref,
     hid_t, q, g, k_all, v_all, kc, vc, kct, qt, gt, qs, gs,
     e0, e1, dp0, dp1, p, mxs, inv, delta, side, low,
-    kv_stage, kv_got, kv_mid, kv_last, pr_stage, pr_got, pr_mid, pr_last,
-    local_sem, gather_send, gather_recv, sum_send, sum_recv,
+    kv_stage, kv_own, kv_got, kv_mid, kv_last, pr_stage, pr_own, pr_got, pr_mid, pr_last,
+    slots, where_to, local_sem, gather_send, gather_recv,
+    sum_send, sum_recv, sum_send_on, sum_recv_on,
 ):
     me, y, x = place()
     def park(c):
@@ -330,6 +319,21 @@
     keys = Gather(k_all, gather_send.at[0], gather_recv.at[0])
     vals = Gather(v_all, gather_send.at[1], gather_recv.at[1])
     keys.own()
+
+    for t in range(2):
+        cur = parents[2 * me + t]
+        for i in range(DEPTH):
+            slots[t, i] = jnp.where(cur >= 0, cur, SEGS)
+            cur = jnp.where(cur >= 0, parents[jnp.maximum(cur, 0)], -1)
+
+    def find(j):
+        for t in range(2):
+            found = jnp.where(j == 2 * me + t, DEPTH, SLOTS)
+            for i in range(DEPTH):
+                found = jnp.where(slots[t, i] == j, i, found)
+            where_to[t, j] = found
+
+    loop(SEGS, find)
 
     locals_[0].wait()
     locals_[1].wait()
@@ -367,45 +371,33 @@
         lambda unit: prob_steps(unit, slots, e, mxs, inv, p),
     )
 
-    def spread(acc, reduce):
-        def put(dest):
-            blocks = []
-            for half in range(2):
-                block = jnp.zeros((SEG, HD), F32)
-                for t in range(2):
-                    block += acc[t, where_to[t, 2 * dest + half]]
-                blocks.append(block)
-            reduce.put(dest, *blocks)
-
-        loop(RANKS, put)
-        reduce.start()
-
-    def make(i, stage, got, mid, last):
-        j = i % 2
-        return Reduce(
-            stage.at[j], got.at[j], mid.at[j], last.at[j], sum_send.at[i], sum_recv.at[i]
-        )
-
-    dv = make(0, kv_stage, kv_got, kv_mid, kv_last)
-    dk = make(1, kv_stage, kv_got, kv_mid, kv_last)
-    pv = make(2, pr_stage, pr_got, pr_mid, pr_last)
-    pk = make(3, pr_stage, pr_got, pr_mid, pr_last)
-
-    def project(reduce, grad, scale):
-        for half, total in enumerate(grad.finish()):
-            low[pl.ds(half * SEG, SEG), :] = (total * scale).astype(BF)
+    def make(i, *buffers):
+        sems = (sum_send, sum_recv, sum_send_on, sum_recv_on)
+        return Reduce(*(b.at[i % 2] for b in buffers), *(sem.at[i] for sem in sems))
+
+    dv = make(0, kv_stage, kv_own, kv_got, kv_mid, kv_last)
+    dk = make(1, kv_stage, kv_own, kv_got, kv_mid, kv_last)
+    pv = make(2, pr_stage, pr_own, pr_got, pr_mid, pr_last)
+    pk = make(3, pr_stage, pr_own, pr_got, pr_mid, pr_last)
+
+    def side_block(rank, half):
+        segment = 2 * rank + half
+        return side[0, where_to[0, segment]] + side[1, where_to[1, segment]]
+
+    def project(reduce, grad, scale, now):
+        for half in range(2):
+            low[pl.ds(half * SEG, SEG), :] = (grad.finish(half) * scale).astype(BF)
         weights = low[...]
 
-        def put(dest):
-            rows = pl.ds(pl.multiple_of(dest * DCOLS, 64), DCOLS)
-            out = dot(hid_t[rows, :], weights)
-            reduce.put(dest, out[: DCOLS // 2], out[DCOLS // 2 :])
-
-        loop(RANKS, put)
+        def block(rank, half):
+            first = rank * DCOLS + half * (DCOLS // 2)
+            return dot(hid_t[pl.ds(pl.multiple_of(first, 32), DCOLS // 2), :], weights)
+
+        reduce.scatter(block, now)
 
     for t in range(2):
         side_grad(t, p, gs, side)
-    spread(side, dv)
+    dv.scatter(side_block)
 
     vals.arrive()
     v_all[SEGS] = jnp.zeros((SEG, HD), BF)
@@ -420,19 +412,18 @@
     dv.middle()
     for t in range(2):
         side_grad(t, p, qs, side)
-    spread(side, dk)
+    dk.scatter(side_block)
     loop(UNITS, lambda u: dq_unit(u, kct, p, dq_ref))
-    project(pv, dv, 1.0)
+    project(pv, dv, 1.0, False)
     dk.middle()
     pv.start()
-    project(pk, dk, SCALE)
-    pk.start()
+    project(pk, dk, SCALE, True)
     pv.middle()
     pk.middle()
-    for half, total in enumerate(pv.finish()):
-        proj_ref[pl.ds(half * (DCOLS // 2), DCOLS // 2), pl.ds(HD, HD)] = total
-    for half, total in enumerate(pk.finish()):
-        proj_ref[pl.ds(half * (DCOLS // 2), DCOLS // 2), pl.ds(0, HD)] = total
+    for half in range(2):
+        rows = pl.ds(half * (DCOLS // 2), DCOLS // 2)
+        proj_ref[rows, pl.ds(HD, HD)] = pv.finish(half)
+        proj_ref[rows, pl.ds(0, HD)] = pk.finish(half)
     for part in (keys, vals, dv, dk, pv, pk):
         part.drain()
 
@@ -471,29 +462,26 @@
         pltpu.VMEM((UNITS, 8, W), F32),
         pltpu.VMEM((2, SLOTS + 1, SEG, HD), F32),
         pltpu.VMEM((tokens, HD), BF),
-        pltpu.VMEM((2, 2, SIDE, SIDE, SEG, HD), BF),
-        pltpu.VMEM((2, 2, 3, SIDE, SEG, HD), BF),
-        pltpu.VMEM((2, 2, SIDE, SEG, HD), BF),
-        pltpu.VMEM((2, 2, 3, SEG, HD), BF),
-        pltpu.VMEM((2, 2, SIDE, SIDE, half, HD), BF),
-        pltpu.VMEM((2, 2, 3, SIDE, half, HD), BF),
-        pltpu.VMEM((2, 2, SIDE, half, HD), BF),
-        pltpu.VMEM((2, 2, 3, half, HD), BF),
+        pltpu.VMEM((2, 2, SIDE - 1, SIDE, SEG, HD), BF),
+        pltpu.VMEM((2, 2, SIDE, SEG, HD), F32),
+        pltpu.VMEM((2, 2, SIDE - 1, SIDE, SEG, HD), BF),
+        pltpu.VMEM((2, 2, SIDE - 1, SEG, HD), BF),
+        pltpu.VMEM((2, 2, SIDE - 1, SEG, HD), BF),
+        pltpu.VMEM((2, 2, SIDE - 1, SIDE, half, HD), BF),
+        pltpu.VMEM((2, 2, SIDE, half, HD), F32),
+        pltpu.VMEM((2, 2, SIDE - 1, SIDE, half, HD), BF),
+        pltpu.VMEM((2, 2, SIDE - 1, half, HD), BF),
+        pltpu.VMEM((2, 2, SIDE - 1, half, HD), BF),
+        pltpu.SMEM((2, DEPTH), jnp.int32),
+        pltpu.SMEM((2, SEGS), jnp.int32),
         pltpu.SemaphoreType.DMA((2 + D // W,)),
         pltpu.SemaphoreType.DMA((2, 2, RANKS)),
         pltpu.SemaphoreType.DMA((2, 2, RANKS)),
-        pltpu.SemaphoreType.DMA((4, 2, 2, SIDE)),
-        pltpu.SemaphoreType.DMA((4, 2, 2, SIDE)),
+        pltpu.SemaphoreType.DMA((4, 2, SIDE, SIDE)),
+        pltpu.SemaphoreType.DMA((4, 2, SIDE, SIDE)),
+        pltpu.SemaphoreType.DMA((4, 2, SIDE)),
+        pltpu.SemaphoreType.DMA((4, 2, SIDE)),
     ]
-    slots, where_to = pl.pallas_call(
-        table_kernel,
-        out_shape=(
-            jax.ShapeDtypeStruct((2, DEPTH), jnp.int32),
-            jax.ShapeDtypeStruct((2, SEGS), jnp.int32),
-        ),
-        in_specs=[smem],
-        out_specs=(smem, smem),
-    )(parents)
     out_shape = (
         jax.ShapeDtypeStruct((tokens, GROUP * HD), BF),
         jax.ShapeDtypeStruct((DCOLS, 2 * HD), F32),
@@ -501,13 +489,13 @@
     grads = pl.pallas_call(
         kernel,
         out_shape=out_shape,
-        in_specs=[hbm, hbm, vmem, vmem, hbm, smem, smem],
+        in_specs=[hbm, hbm, vmem, vmem, hbm, smem],
         out_specs=(vmem, vmem),
         scratch_shapes=scratch,
         compiler_params=pltpu.CompilerParams(
             collective_id=1, has_side_effects=True, vmem_limit_bytes=62 << 20
         ),
-    )(hidden_in, queries, keys, values, out_grad, slots, where_to)
+    )(hidden_in, queries, keys, values, out_grad, parents)
     return pl.pallas_call(
         copy_kernel,
         out_shape=out_shape,

time: 76 us -> 72.1 us (0.949)
  Pallas kernels: 75.2 us -> 71.3 us
    pallas_call x1 -> x0, Pallas kernels: 2.46 us -> none  [on_device(): pl.pallas_call(table_kernel, out_shape=(jax.ShapeDtypeStruct((2, DEPTH),...]
    pallas_call x1, Pallas kernels: 70.7 us -> 69.2 us  [on_device(): pl.pallas_call(kernel, out_shape=out_shape, in_specs=[hbm, hbm, vmem, vme...]
where the time goes in v3:
time: 72.1 us; the launch traced here: 71.9 us
  Pallas kernels  71.3 us (99%)
    pallas_call x1, Pallas kernels, on_device(): pl.pallas_call(kernel, out_shape=out_shape, in_specs=[hbm, hbm, vmem, vme...  69.2 us
    pallas_call x1, Pallas kernels, on_device(): pl.pallas_call(copy_kernel, out_shape=out_shape, in_specs=[vmem, vmem], o...  2.06 us

profile of v3, /device:TPU:0, one launch (start us, length us, event | category | flops | bytes accessed | tf_op | source)
XLA Modules:
  0.0 71.9 jit_solution(11917039159766380700)
XLA Ops:
  0.6 69.2 %shard_map.77 = (bf16[256,1024]{1,0:T(8,128)(2,1)}, f32[320,256]{1,0:T(8,128)}) custom-call(bf16[256,5120]{1,0:T(8,128)(2,1)} %hid_ref.1, bf16[256,1024]{1,0:T(8,128)(2,1)} %q_ref.1, bf16[256,128]{1,0:T(8,128)(2,1)} %k_ref.1, bf16[256,128]{1,0:T(8,128)(2,1)} %v_ref.1, bf16[256,1024]{1,0:T(8,128)(2,1)} %g_ref.1, s32[32]{0:T(128)} %parents.1), custom_call_target="tpu_custom_call" | custom-call | tf_op jit(solution)/shard_map/pallas_call | solution.py:489
  69.9 2.1 %shard_map.78 = (bf16[256,1024]{1,0:T(8,128)(2,1)}, f32[320,256]{1,0:T(8,128)}) custom-call(bf16[256,1024]{1,0:T(8,128)(2,1)} %get-tuple-element.4.dq_in, f32[320,256]{1,0:T(8,128)} %get-tuple-element.5.proj_in), custom_call_target="tpu_custom_call" | custom-call | tf_op jit(solution)/shard_map/pallas_call | solution.py:499

commit v4 on v3

--- a/solution.py
+++ b/solution.py
@@ -220,7 +220,7 @@
         self.send, self.recv, self.send_on, self.recv_on = send, recv, send_on, recv_on
         self.first, self.second = {}, {}
 
-    def scatter(self, block, now=True):
+    def scatter(self, block):
         _, y, x = place()
         for step in (*STEPS, 0):
             for half in range(2):
@@ -241,24 +241,23 @@
                         self.recv.at[half, step, j],
                         (at(0, step), at(step, 0))[half],
                     )
+                    copy.start()
                     self.first[half, step, j] = copy
-                    if now:
-                        copy.start()
-
-    def start(self):
-        for copy in self.first.values():
-            copy.start()
+
+    def total(self, half, j, k):
+        for step in STEPS:
+            self.first[half, step, j].wait_recv()
+        total = self.own[half, k]
+        for step in STEPS:
+            total += self.got[half, step - 1, k].astype(F32)
+        return total
 
     def middle(self):
         _, y, x = place()
         for j in range(SIDE):
             for half in range(2):
                 k = lax.rem((y, x)[half] + 1 + j, SIDE)
-                for step in STEPS:
-                    self.first[half, step, j].wait_recv()
-                total = self.own[half, k]
-                for step in STEPS:
-                    total += self.got[half, step - 1, k].astype(F32)
+                total = self.total(half, j, k)
                 if j == SIDE - 1:
                     self.own[half, k] = total
                     continue
@@ -286,14 +285,88 @@
             copy.wait_send()
 
 
+class Hidden:
+    def __init__(self, hid_t, got, send, recv):
+        self.hid_t, self.got, self.send, self.recv = hid_t, got, send, recv
+        self.copies, self.here = {}, set()
+
+    def rows(self, column, k, half):
+        rank = k * SIDE + column if half == 0 else column * SIDE + k
+        first = rank * DCOLS + half * (DCOLS // 2)
+        return pl.ds(pl.multiple_of(first, 32), DCOLS // 2)
+
+    def start(self):
+        _, y, x = place()
+        for step in STEPS:
+            for half in range(2):
+                mine, other = ((x, y), (y, x))[half]
+                for j in range(SIDE):
+                    k = lax.rem(other + 1 + j, SIDE)
+                    copy = remote(
+                        self.hid_t.at[self.rows(lax.rem(mine + step, SIDE), k, half), :],
+                        self.got.at[half, step - 1, k],
+                        self.send.at[half, step, j],
+                        self.recv.at[half, step, j],
+                        (at(0, step), at(step, 0))[half],
+                    )
+                    copy.start()
+                    self.copies[half, step, j] = copy
+
+    def blocks(self, half, j, k):
+        _, y, x = place()
+        if (half, j) not in self.here:
+            self.here.add((half, j))
+            for step in STEPS:
+                self.copies[half, step, j].wait_recv()
+        own = self.hid_t[self.rows((x, y)[half], k, half), :]
+        return [own, *(self.got[half, step - 1, k] for step in STEPS)]
+
+    def drain(self):
+        for copy in self.copies.values():
+            copy.wait_send()
+
+
+class Project(Reduce):
+    def __init__(self, hidden, low, low_got, share_send, share_recv, own, mid, last, *sems):
+        super().__init__(None, own, None, mid, last, None, None, *sems)
+        self.hidden, self.low, self.low_got = hidden, low, low_got
+        self.share_send, self.share_recv = share_send, share_recv
+
+    def share(self, grad, scale):
+        for half in range(2):
+            self.low[pl.ds(half * SEG, SEG), :] = (grad.finish(half) * scale).astype(BF)
+        for step in STEPS:
+            for half in range(2):
+                copy = remote(
+                    self.low,
+                    self.low_got.at[half, step - 1],
+                    self.share_send.at[half, step],
+                    self.share_recv.at[half, step],
+                    (at(0, step), at(step, 0))[half],
+                )
+                copy.start()
+                self.first[half, step] = copy
+
+    def total(self, half, j, k):
+        if j == 0:
+            for step in STEPS:
+                self.first[half, step].wait_recv()
+        blocks = self.hidden.blocks(half, j, k)
+        total = dot(blocks[0], self.low[...])
+        for step, block in zip(STEPS, blocks[1:]):
+            total += dot(block, self.low_got[half, step - 1])
+        return total
+
+
 def kernel(
     hid_ref, q_ref, k_ref, v_ref, g_ref, parents,
     dq_ref, proj_ref,
     hid_t, q, g, k_all, v_all, kc, vc, kct, qt, gt, qs, gs,
-    e0, e1, dp0, dp1, p, mxs, inv, delta, side, low,
-    kv_stage, kv_own, kv_got, kv_mid, kv_last, pr_stage, pr_own, pr_got, pr_mid, pr_last,
+    e0, e1, dp0, dp1, p, mxs, inv, delta, side, low, low_got,
+    kv_stage, kv_own, kv_got, kv_mid, kv_last, hid_got, pr_own, pr_mid, pr_last,
     slots, where_to, local_sem, gather_send, gather_recv,
     sum_send, sum_recv, sum_send_on, sum_recv_on,
+    hid_send, hid_recv, share_send, share_recv,
 ):
     me, y, x = place()
     def park(c):
@@ -359,6 +432,8 @@
 
     e, dp = (e0, e1), (dp0, dp1)
     keys.arrive()
+    hidden = Hidden(hid_t, hid_got, hid_send, hid_recv)
+    hidden.start()
     for t in range(2):
         head = k_all[2 * me + t, 0:16, :].astype(F32)[0:1]
         k_all[SEGS] = jnp.broadcast_to(head, (SEG, HD)).astype(BF)
@@ -371,29 +446,23 @@
         lambda unit: prob_steps(unit, slots, e, mxs, inv, p),
     )
 
-    def make(i, *buffers):
-        sems = (sum_send, sum_recv, sum_send_on, sum_recv_on)
-        return Reduce(*(b.at[i % 2] for b in buffers), *(sem.at[i] for sem in sems))
-
-    dv = make(0, kv_stage, kv_own, kv_got, kv_mid, kv_last)
-    dk = make(1, kv_stage, kv_own, kv_got, kv_mid, kv_last)
-    pv = make(2, pr_stage, pr_own, pr_got, pr_mid, pr_last)
-    pk = make(3, pr_stage, pr_own, pr_got, pr_mid, pr_last)
+    def sums(i):
+        buffers = (kv_stage, kv_own, kv_got, kv_mid, kv_last)
+        return Reduce(
+            *(b.at[i] for b in (*buffers, sum_send, sum_recv)), sum_send_on.at[i], sum_recv_on.at[i]
+        )
+
+    def project(i):
+        buffers = (low, low_got, share_send, share_recv, pr_own, pr_mid, pr_last)
+        return Project(
+            hidden, *(b.at[i] for b in buffers), sum_send_on.at[2 + i], sum_recv_on.at[2 + i]
+        )
+
+    dv, dk, pv, pk = sums(0), sums(1), project(0), project(1)
 
     def side_block(rank, half):
         segment = 2 * rank + half
         return side[0, where_to[0, segment]] + side[1, where_to[1, segment]]
-
-    def project(reduce, grad, scale, now):
-        for half in range(2):
-            low[pl.ds(half * SEG, SEG), :] = (grad.finish(half) * scale).astype(BF)
-        weights = low[...]
-
-        def block(rank, half):
-            first = rank * DCOLS + half * (DCOLS // 2)
-            return dot(hid_t[pl.ds(pl.multiple_of(first, 32), DCOLS // 2), :], weights)
-
-        reduce.scatter(block, now)
 
     for t in range(2):
         side_grad(t, p, gs, side)
@@ -409,22 +478,21 @@
         lambda unit: dprob_steps(unit, vc, gt, e, inv, dp, delta),
         lambda unit: dscore_steps(unit, e, inv, dp, delta, p),
     )
-    dv.middle()
     for t in range(2):
         side_grad(t, p, qs, side)
     dk.scatter(side_block)
     loop(UNITS, lambda u: dq_unit(u, kct, p, dq_ref))
-    project(pv, dv, 1.0, False)
+    dv.middle()
     dk.middle()
-    pv.start()
-    project(pk, dk, SCALE, True)
+    pv.share(dv, 1.0)
+    pk.share(dk, SCALE)
     pv.middle()
     pk.middle()
     for half in range(2):
         rows = pl.ds(half * (DCOLS // 2), DCOLS // 2)
         proj_ref[rows, pl.ds(HD, HD)] = pv.finish(half)
         proj_ref[rows, pl.ds(0, HD)] = pk.finish(half)
-    for part in (keys, vals, dv, dk, pv, pk):
+    for part in (keys, vals, hidden, dv, dk, pv, pk):
         part.drain()
 
 
@@ -461,15 +529,15 @@
         pltpu.VMEM((UNITS, 8, W), F32),
         pltpu.VMEM((UNITS, 8, W), F32),
         pltpu.VMEM((2, SLOTS + 1, SEG, HD), F32),
-        pltpu.VMEM((tokens, HD), BF),
+        pltpu.VMEM((2, tokens, HD), BF),
+        pltpu.VMEM((2, 2, SIDE - 1, tokens, HD), BF),
         pltpu.VMEM((2, 2, SIDE - 1, SIDE, SEG, HD), BF),
         pltpu.VMEM((2, 2, SIDE, SEG, HD), F32),
         pltpu.VMEM((2, 2, SIDE - 1, SIDE, SEG, HD), BF),
         pltpu.VMEM((2, 2, SIDE - 1, SEG, HD), BF),
         pltpu.VMEM((2, 2, SIDE - 1, SEG, HD), BF),
-        pltpu.VMEM((2, 2, SIDE - 1, SIDE, half, HD), BF),
+        pltpu.VMEM((2, SIDE - 1, SIDE, half, tokens), BF),
         pltpu.VMEM((2, 2, SIDE, half, HD), F32),
-        pltpu.VMEM((2, 2, SIDE - 1, SIDE, half, HD), BF),
         pltpu.VMEM((2, 2, SIDE - 1, half, HD), BF),
         pltpu.VMEM((2, 2, SIDE - 1, half, HD), BF),
         pltpu.SMEM((2, DEPTH), jnp.int32),
@@ -477,10 +545,14 @@
         pltpu.SemaphoreType.DMA((2 + D // W,)),
         pltpu.SemaphoreType.DMA((2, 2, RANKS)),
         pltpu.SemaphoreType.DMA((2, 2, RANKS)),
-        pltpu.SemaphoreType.DMA((4, 2, SIDE, SIDE)),
-        pltpu.SemaphoreType.DMA((4, 2, SIDE, SIDE)),
+        pltpu.SemaphoreType.DMA((2, 2, SIDE, SIDE)),
+        pltpu.SemaphoreType.DMA((2, 2, SIDE, SIDE)),
         pltpu.SemaphoreType.DMA((4, 2, SIDE)),
         pltpu.SemaphoreType.DMA((4, 2, SIDE)),
+        pltpu.SemaphoreType.DMA((2, SIDE, SIDE)),
+        pltpu.SemaphoreType.DMA((2, SIDE, SIDE)),
+        pltpu.SemaphoreType.DMA((2, 2, SIDE)),
+        pltpu.SemaphoreType.DMA((2, 2, SIDE)),
     ]
     out_shape = (
         jax.ShapeDtypeStruct((tokens, GROUP * HD), BF),

time: 72.1 us -> 70.5 us (0.978)
  Pallas kernels: 71.3 us -> 69.7 us
    pallas_call x1, Pallas kernels: 69.2 us -> 67.7 us  [on_device(): pl.pallas_call(kernel, out_shape=out_shape, in_specs=[hbm, hbm, vmem, vme...]
where the time goes in v4:
time: 70.5 us; the launch traced here: 70.4 us
  Pallas kernels  69.7 us (99%)
    pallas_call x1, Pallas kernels, on_device(): pl.pallas_call(kernel, out_shape=out_shape, in_specs=[hbm, hbm, vmem, vme...  67.7 us
    pallas_call x1, Pallas kernels, on_device(): pl.pallas_call(copy_kernel, out_shape=out_shape, in_specs=[vmem, vmem], o...  2.06 us

profile of v4, /device:TPU:0, one launch (start us, length us, event | category | flops | bytes accessed | tf_op | source)
XLA Modules:
  0.0 70.4 jit_solution(3475076054366128230)
XLA Ops:
  0.6 67.7 %shard_map.77 = (bf16[256,1024]{1,0:T(8,128)(2,1)}, f32[320,256]{1,0:T(8,128)}) custom-call(bf16[256,5120]{1,0:T(8,128)(2,1)} %hid_ref.1, bf16[256,1024]{1,0:T(8,128)(2,1)} %q_ref.1, bf16[256,128]{1,0:T(8,128)(2,1)} %k_ref.1, bf16[256,128]{1,0:T(8,128)(2,1)} %v_ref.1, bf16[256,1024]{1,0:T(8,128)(2,1)} %g_ref.1, s32[32]{0:T(128)} %parents.1), custom_call_target="tpu_custom_call" | custom-call | tf_op jit(solution)/shard_map/pallas_call | solution.py:561
  68.3 2.1 %shard_map.78 = (bf16[256,1024]{1,0:T(8,128)(2,1)}, f32[320,256]{1,0:T(8,128)}) custom-call(bf16[256,1024]{1,0:T(8,128)(2,1)} %get-tuple-element.4.dq_in, f32[320,256]{1,0:T(8,128)} %get-tuple-element.5.proj_in), custom_call_target="tpu_custom_call" | custom-call | tf_op jit(solution)/shard_map/pallas_call | solution.py:571

commit v5 on v4

--- a/solution.py
+++ b/solution.py
@@ -26,6 +26,7 @@
 SCALE = HD ** -0.5
 PEN = 1e30
 STEPS = (1, 3, 2)
+NEAR, FAR = (1, 3), 2
 
 
 def dot(a, b):
@@ -290,36 +291,29 @@
         self.hid_t, self.got, self.send, self.recv = hid_t, got, send, recv
         self.copies, self.here = {}, set()
 
-    def rows(self, column, k, half):
-        rank = k * SIDE + column if half == 0 else column * SIDE + k
-        first = rank * DCOLS + half * (DCOLS // 2)
-        return pl.ds(pl.multiple_of(first, 32), DCOLS // 2)
-
-    def start(self):
+    def start(self, step):
         _, y, x = place()
-        for step in STEPS:
-            for half in range(2):
-                mine, other = ((x, y), (y, x))[half]
-                for j in range(SIDE):
-                    k = lax.rem(other + 1 + j, SIDE)
-                    copy = remote(
-                        self.hid_t.at[self.rows(lax.rem(mine + step, SIDE), k, half), :],
-                        self.got.at[half, step - 1, k],
-                        self.send.at[half, step, j],
-                        self.recv.at[half, step, j],
-                        (at(0, step), at(step, 0))[half],
-                    )
-                    copy.start()
-                    self.copies[half, step, j] = copy
-
-    def blocks(self, half, j, k):
+        for half in range(2):
+            column = lax.rem((x, y)[half] + step, SIDE)
+            src = (self.hid_t.at[0, :, column], self.hid_t.at[1, column])[half]
+            copy = remote(
+                src,
+                self.got.at[half, step // 2],
+                self.send.at[half, step],
+                self.recv.at[half, step],
+                (at(0, step), at(step, 0))[half],
+            )
+            copy.start()
+            self.copies[half, step] = copy
+
+    def blocks(self, half, k):
         _, y, x = place()
-        if (half, j) not in self.here:
-            self.here.add((half, j))
-            for step in STEPS:
-                self.copies[half, step, j].wait_recv()
-        own = self.hid_t[self.rows((x, y)[half], k, half), :]
-        return [own, *(self.got[half, step - 1, k] for step in STEPS)]
+        if half not in self.here:
+            self.here.add(half)
+            for step in NEAR:
+                self.copies[half, step].wait_recv()
+        own = self.hid_t[(0, k, x) if half == 0 else (1, y, k)]
+        return [own, *(self.got[half, step // 2, k] for step in NEAR)]
 
     def drain(self):
         for copy in self.copies.values():
@@ -327,35 +321,40 @@
 
 
 class Project(Reduce):
-    def __init__(self, hidden, low, low_got, share_send, share_recv, own, mid, last, *sems):
-        super().__init__(None, own, None, mid, last, None, None, *sems)
+    def __init__(self, hidden, low, low_got, share_send, share_recv, stage, own, got, mid, last, *sems):
+        super().__init__(stage, own, got, mid, last, None, None, *sems)
         self.hidden, self.low, self.low_got = hidden, low, low_got
         self.share_send, self.share_recv = share_send, share_recv
 
     def share(self, grad, scale):
         for half in range(2):
             self.low[pl.ds(half * SEG, SEG), :] = (grad.finish(half) * scale).astype(BF)
-        for step in STEPS:
+        for step in NEAR:
             for half in range(2):
-                copy = remote(
-                    self.low,
-                    self.low_got.at[half, step - 1],
-                    self.share_send.at[half, step],
-                    self.share_recv.at[half, step],
-                    (at(0, step), at(step, 0))[half],
-                )
-                copy.start()
-                self.first[half, step] = copy
+                self.send_first(half, step, self.low, self.low_got.at[half, step // 2])
+        _, y, x = place()
+        for half in range(2):
+            column = lax.rem((x, y)[half] + FAR, SIDE)
+            for k in range(SIDE):
+                block = self.hidden.hid_t[(0, k, column) if half == 0 else (1, column, k)]
+                self.stage[half, k] = dot(block, self.low[...]).astype(BF)
+            self.send_first(half, FAR, self.stage.at[half], self.got.at[half])
+
+    def send_first(self, half, step, src, dst):
+        sems = self.share_send.at[half, step], self.share_recv.at[half, step]
+        copy = remote(src, dst, *sems, (at(0, step), at(step, 0))[half])
+        copy.start()
+        self.first[half, step] = copy
 
     def total(self, half, j, k):
         if j == 0:
             for step in STEPS:
                 self.first[half, step].wait_recv()
-        blocks = self.hidden.blocks(half, j, k)
+        blocks = self.hidden.blocks(half, k)
         total = dot(blocks[0], self.low[...])
-        for step, block in zip(STEPS, blocks[1:]):
-            total += dot(block, self.low_got[half, step - 1])
-        return total
+        for step, block in zip(NEAR, blocks[1:]):
+            total += dot(block, self.low_got[half, step // 2])
+        return total + self.got[half, k].astype(F32)
 
 
 def kernel(
@@ -363,7 +362,7 @@
     dq_ref, proj_ref,
     hid_t, q, g, k_all, v_all, kc, vc, kct, qt, gt, qs, gs,
     e0, e1, dp0, dp1, p, mxs, inv, delta, side, low, low_got,
-    kv_stage, kv_own, kv_got, kv_mid, kv_last, hid_got, pr_own, pr_mid, pr_last,
+    kv_stage, kv_own, kv_got, kv_mid, kv_last, hid_got, pr_stage, pr_own, pr_got, pr_mid, pr_last,
     slots, where_to, local_sem, gather_send, gather_recv,
     sum_send, sum_recv, sum_send_on, sum_recv_on,
     hid_send, hid_recv, share_send, share_recv,
@@ -424,16 +423,25 @@
     loop(UNITS, prepare)
     keys.forward()
     vals.own()
-    vals.forward()
-
     for c in range(D // W):
         locals_[2 + c].wait()
-        hid_t[pl.ds(c * W, W), :] = park(c)[...].T
+        turned = park(c)[...].T
+        first = c * W
+        while first < (c + 1) * W:
+            block, start = divmod(first, DCOLS // 2)
+            size = min(DCOLS // 2 - start, (c + 1) * W - first)
+            rank, half = divmod(block, 2)
+            hid_t[half, rank // SIDE, rank % SIDE, pl.ds(start, size), :] = turned[
+                first - c * W : first - c * W + size
+            ]
+            first += size
 
     e, dp = (e0, e1), (dp0, dp1)
+    hidden = Hidden(hid_t, hid_got, hid_send, hid_recv)
+    vals.forward()
     keys.arrive()
-    hidden = Hidden(hid_t, hid_got, hid_send, hid_recv)
-    hidden.start()
+    hidden.start(1)
+    hidden.start(3)
     for t in range(2):
         head = k_all[2 * me + t, 0:16, :].astype(F32)[0:1]
         k_all[SEGS] = jnp.broadcast_to(head, (SEG, HD)).astype(BF)
@@ -453,7 +461,7 @@
         )
 
     def project(i):
-        buffers = (low, low_got, share_send, share_recv, pr_own, pr_mid, pr_last)
+        buffers = (low, low_got, share_send, share_recv, pr_stage, pr_own, pr_got, pr_mid, pr_last)
         return Project(
             hidden, *(b.at[i] for b in buffers), sum_send_on.at[2 + i], sum_recv_on.at[2 + i]
         )
@@ -508,7 +516,7 @@
     tokens = 2 * SEG
     half = DCOLS // 2
     scratch = [
-        pltpu.VMEM((D, tokens), BF),
+        pltpu.VMEM((2, SIDE, SIDE, half, tokens), BF),
         pltpu.VMEM((tokens, GROUP * HD), BF),
         pltpu.VMEM((tokens, GROUP * HD), BF),
         pltpu.VMEM((SEGS + 1, SEG, HD), BF),
@@ -530,14 +538,16 @@
         pltpu.VMEM((UNITS, 8, W), F32),
         pltpu.VMEM((2, SLOTS + 1, SEG, HD), F32),
         pltpu.VMEM((2, tokens, HD), BF),
-        pltpu.VMEM((2, 2, SIDE - 1, tokens, HD), BF),
+        pltpu.VMEM((2, 2, 2, tokens, HD), BF),
         pltpu.VMEM((2, 2, SIDE - 1, SIDE, SEG, HD), BF),
         pltpu.VMEM((2, 2, SIDE, SEG, HD), F32),
         pltpu.VMEM((2, 2, SIDE - 1, SIDE, SEG, HD), BF),
         pltpu.VMEM((2, 2, SIDE - 1, SEG, HD), BF),
         pltpu.VMEM((2, 2, SIDE - 1, SEG, HD), BF),
-        pltpu.VMEM((2, SIDE - 1, SIDE, half, tokens), BF),
+        pltpu.VMEM((2, 2, SIDE, half, tokens), BF),
+        pltpu.VMEM((2, 2, SIDE, half, HD), BF),
         pltpu.VMEM((2, 2, SIDE, half, HD), F32),
+        pltpu.VMEM((2, 2, SIDE, half, HD), BF),
         pltpu.VMEM((2, 2, SIDE - 1, half, HD), BF),
         pltpu.VMEM((2, 2, SIDE - 1, half, HD), BF),
         pltpu.SMEM((2, DEPTH), jnp.int32),
@@ -549,8 +559,8 @@
         pltpu.SemaphoreType.DMA((2, 2, SIDE, SIDE)),
         pltpu.SemaphoreType.DMA((4, 2, SIDE)),
         pltpu.SemaphoreType.DMA((4, 2, SIDE)),
-        pltpu.SemaphoreType.DMA((2, SIDE, SIDE)),
-        pltpu.SemaphoreType.DMA((2, SIDE, SIDE)),
+        pltpu.SemaphoreType.DMA((2, SIDE)),
+        pltpu.SemaphoreType.DMA((2, SIDE)),
         pltpu.SemaphoreType.DMA((2, 2, SIDE)),
         pltpu.SemaphoreType.DMA((2, 2, SIDE)),
     ]

time: 70.5 us -> 68.2 us (0.967)
  Pallas kernels: 69.7 us -> 67.2 us
    pallas_call x1, Pallas kernels: 67.7 us -> 65.1 us  [on_device(): pl.pallas_call(kernel, out_shape=out_shape, in_specs=[hbm, hbm, vmem, vme...]
where the time goes in v5:
time: 68.2 us; the launch traced here: 67.8 us
  Pallas kernels  67.2 us (99%)
    pallas_call x1, Pallas kernels, on_device(): pl.pallas_call(kernel, out_shape=out_shape, in_specs=[hbm, hbm, vmem, vme...  65.1 us
    pallas_call x1, Pallas kernels, on_device(): pl.pallas_call(copy_kernel, out_shape=out_shape, in_specs=[vmem, vmem], o...  2.06 us

profile of v5, /device:TPU:0, one launch (start us, length us, event | category | flops | bytes accessed | tf_op | source)
XLA Modules:
  0.0 67.8 jit_solution(5509874450827003813)
XLA Ops:
  0.6 65.1 %shard_map.77 = (bf16[256,1024]{1,0:T(8,128)(2,1)}, f32[320,256]{1,0:T(8,128)}) custom-call(bf16[256,5120]{1,0:T(8,128)(2,1)} %hid_ref.1, bf16[256,1024]{1,0:T(8,128)(2,1)} %q_ref.1, bf16[256,128]{1,0:T(8,128)(2,1)} %k_ref.1, bf16[256,128]{1,0:T(8,128)(2,1)} %v_ref.1, bf16[256,1024]{1,0:T(8,128)(2,1)} %g_ref.1, s32[32]{0:T(128)} %parents.1), custom_call_target="tpu_custom_call" | custom-call | tf_op jit(solution)/shard_map/pallas_call | solution.py:571
  65.8 2.1 %shard_map.78 = (bf16[256,1024]{1,0:T(8,128)(2,1)}, f32[320,256]{1,0:T(8,128)}) custom-call(bf16[256,1024]{1,0:T(8,128)(2,1)} %get-tuple-element.4.dq_in, f32[320,256]{1,0:T(8,128)} %get-tuple-element.5.proj_in), custom_call_target="tpu_custom_call" | custom-call | tf_op jit(solution)/shard_map/pallas_call | solution.py:581

commit v6 on v5

--- a/solution.py
+++ b/solution.py
@@ -223,11 +223,11 @@
 
     def scatter(self, block):
         _, y, x = place()
-        for step in (*STEPS, 0):
-            for half in range(2):
-                mine, other = ((x, y), (y, x))[half]
-                column = lax.rem(mine + step, SIDE)
-                for j in range(SIDE):
+        for j in range(SIDE):
+            for step in (*STEPS, 0):
+                for half in range(2):
+                    mine, other = ((x, y), (y, x))[half]
+                    column = lax.rem(mine + step, SIDE)
                     k = lax.rem(other + 1 + j, SIDE)
                     rank = k * SIDE + column if half == 0 else column * SIDE + k
                     value = block(rank, half)
@@ -489,10 +489,11 @@
     for t in range(2):
         side_grad(t, p, qs, side)
     dk.scatter(side_block)
-    loop(UNITS, lambda u: dq_unit(u, kct, p, dq_ref))
+    loop(UNITS // 2, lambda u: dq_unit(u, kct, p, dq_ref))
     dv.middle()
     dk.middle()
     pv.share(dv, 1.0)
+    loop(UNITS // 2, lambda u: dq_unit(u + UNITS // 2, kct, p, dq_ref))
     pk.share(dk, SCALE)
     pv.middle()
     pk.middle()

time: 68.2 us -> 66.5 us (0.975)
  Pallas kernels: 67.2 us -> 65.7 us
    pallas_call x1, Pallas kernels: 65.1 us -> 63.6 us  [on_device(): pl.pallas_call(kernel, out_shape=out_shape, in_specs=[hbm, hbm, vmem, vme...]
where the time goes in v6:
time: 66.5 us; the launch traced here: 66.3 us
  Pallas kernels  65.7 us (99%)
    pallas_call x1, Pallas kernels, on_device(): pl.pallas_call(kernel, out_shape=out_shape, in_specs=[hbm, hbm, vmem, vme...  63.6 us
    pallas_call x1, Pallas kernels, on_device(): pl.pallas_call(copy_kernel, out_shape=out_shape, in_specs=[vmem, vmem], o...  2.06 us

profile of v6, /device:TPU:0, one launch (start us, length us, event | category | flops | bytes accessed | tf_op | source)
XLA Modules:
  0.0 66.3 jit_solution(1653520050928963497)
XLA Ops:
  0.6 63.6 %shard_map.77 = (bf16[256,1024]{1,0:T(8,128)(2,1)}, f32[320,256]{1,0:T(8,128)}) custom-call(bf16[256,5120]{1,0:T(8,128)(2,1)} %hid_ref.1, bf16[256,1024]{1,0:T(8,128)(2,1)} %q_ref.1, bf16[256,128]{1,0:T(8,128)(2,1)} %k_ref.1, bf16[256,128]{1,0:T(8,128)(2,1)} %v_ref.1, bf16[256,1024]{1,0:T(8,128)(2,1)} %g_ref.1, s32[32]{0:T(128)} %parents.1), custom_call_target="tpu_custom_call" | custom-call | tf_op jit(solution)/shard_map/pallas_call | solution.py:572
  64.3 2.1 %shard_map.78 = (bf16[256,1024]{1,0:T(8,128)(2,1)}, f32[320,256]{1,0:T(8,128)}) custom-call(bf16[256,1024]{1,0:T(8,128)(2,1)} %get-tuple-element.4.dq_in, f32[320,256]{1,0:T(8,128)} %get-tuple-element.5.proj_in), custom_call_target="tpu_custom_call" | custom-call | tf_op jit(solution)/shard_map/pallas_call | solution.py:582
